TPU v7x, 256 devices: a whole 4x4x8 slice. The times are simulated.
256 devices in a mesh: dp: 8 (over y, core), et: 32 (over z, x).
Axes of the slice: x: 4, y: 4, z: 8, core: 2. Of those that a mesh axis runs over, the one named last changes fastest.
Arguments:
- tokens: bfloat16 [1024, 4096], P('dp'), may hold values from -6 to 6
- routed_experts: int32 [1024, 2], P('dp'), may hold values from 0 to 7, all different within a row; in each aligned block of 128 rows (0 to 127, 128 to 255, ...) at most 64 rows name the same one
- choice_weights: float32 [1024, 2], P('dp'), may hold values from 0.1 to 0.9
- gate_up_weight: bfloat16 [2, 4096, 86016], P(None, None, ('et', 'dp')), may hold values from -0.09375 to 0.09375
- down_weight: bfloat16 [86016, 4096], P(('et', 'dp')), may hold values from -0.0625 to 0.0625
- adapter_first_factors: bfloat16 [2, 4096, 512], P(None, 'dp'), may hold values from -0.09375 to 0.09375
- adapter_second_factors: bfloat16 [2, 64, 86016], P(None, None, ('et', 'dp')), may hold values from -0.75 to 0.75
- cotangent: bfloat16 [1024, 4096], P('dp'), may hold values from -6 to 6
Outputs:
- mixed: bfloat16 [1024, 4096], P('dp', 'et')
- token_gradient: bfloat16 [1024, 4096], P('dp', 'et')
- first_factors_gradient: float32 [2, 4096, 512], P(None, 'dp', 'et')
- second_factors_gradient: float32 [2, 64, 86016], P(None, None, ('et', 'dp'))
Inputs may be any that keep to these rules, and one draw needn't show every extreme that they name: `routed_experts`: each token names two different experts. Within the tokens of one index of dp (aligned blocks of 128 rows) no expert is named by more than 64 tokens, and in some block one expert is named by exactly 64.
All inputs are finite; a program needn't handle non-finite values.
Results may differ from a plain program's by a relative error of at most 0.024.
Values may be sent and summed in bfloat16 or wider, within the bound.
No kernel may reach another device: no remote copies, remote signals or barrier semaphores. Data moves between devices by JAX's collectives and lax.ppermute only.
A program may use at most 128 MiB of HBM per device.

v0:
```python
import functools

import jax
import jax.numpy as jnp
from jax import lax
from jax.experimental import pallas as pl
from jax.experimental.pallas import tpu as pltpu
from jax.sharding import Mesh, PartitionSpec as P

ADAPTER_SCALE = 0.5
BF = jnp.bfloat16
F32 = jnp.float32


NT = (((1,), (1,)), ((), ()))
TN = (((0,), (0,)), ((), ()))
NN = (((1,), (0,)), ((), ()))
VMEM = pl.BlockSpec(memory_space=pltpu.VMEM)
HBM = pl.BlockSpec(memory_space=pl.ANY)
SMEM = pl.BlockSpec(memory_space=pltpu.SMEM)


def dot(a, b, dims=NN):
    return lax.dot_general(a, b, dims, preferred_element_type=F32)


def shape(dims, dtype=BF):
    return jax.ShapeDtypeStruct(dims, dtype)


def call(kernel, out_shape, inputs, in_specs, out_specs, scratch=(), name=None, limit=60, flops=0):
    return pl.pallas_call(
        kernel,
        out_shape=out_shape,
        in_specs=in_specs,
        out_specs=out_specs,
        scratch_shapes=list(scratch),
        compiler_params=pltpu.CompilerParams(vmem_limit_bytes=limit * 1024 * 1024),
        cost_estimate=pl.CostEstimate(flops=flops, bytes_accessed=0, transcendentals=0),
        name=name,
    )(*inputs)


def start(source, target, sem):
    copy = pltpu.make_async_copy(source, target, sem)
    copy.start()
    return copy


def tie(value, *earlier):
    return lax.optimization_barrier((value, *earlier))[0]


def swap(values):
    return lax.ppermute(values, "core", [(0, 1), (1, 0)])


def ahead(values, step=1):
    n_y = lax.axis_size("y")
    pairs = [(2 * y + c, 2 * ((y + step * (1 - 2 * c)) % n_y) + c) for y in range(n_y) for c in range(2)]
    return lax.ppermute(values, ("y", "core"), pairs)


def crossed(values, step, first):
    n_y, n_x = lax.axis_size("y"), lax.axis_size("x")
    pairs = []
    for y in range(n_y):
        for c in range(2):
            for x in range(n_x):
                to = ((y + step * (1 - 2 * c)) % n_y, x) if c == first else (y, (x + step) % n_x)
                pairs.append(((y * 2 + c) * n_x + x, (to[0] * 2 + c) * n_x + to[1]))
    return lax.ppermute(values, ("y", "core", "x"), pairs)


def rows_kernel(
    rank, place, tokens, cotangent, first, experts, values, out_o, far_o, gate_o, tokens_v, cotangent_v, first_v, out, sems
):
    copies = [
        start(a, b, sems.at[i])
        for i, (a, b) in enumerate(((first, first_v), (tokens, tokens_v), (cotangent, cotangent_v)))
    ]
    cap, extra = gate_o.shape[0], far_o.shape[0]
    count = 2 * cap
    hits = [experts[j : j + 1, :] == place[3] for j in range(2)]
    weight = sum(jnp.where(hit, values[j : j + 1, :], 0.0) for j, hit in enumerate(hits))
    named = jnp.where(hits[0] | hits[1], 1.0, 0.0)
    before = lax.broadcasted_iota(jnp.int32, (count, count), 0) < lax.broadcasted_iota(jnp.int32, (count, count), 1)
    placed = dot(jnp.broadcast_to(named, (8, count)).astype(BF), jnp.where(before, 1.0, 0.0).astype(BF))[:1, :]
    slot = lax.broadcasted_iota(jnp.int32, (cap, count), 0)
    match = (jnp.broadcast_to(placed, (cap, count)).astype(jnp.int32) == slot) & (
        jnp.broadcast_to(named, (cap, count)) > 0.5
    )
    gate = jnp.sum(jnp.where(match, jnp.broadcast_to(weight, (cap, count)), 0.0), axis=1, keepdims=True)
    gate_o[...] = gate
    pick = jnp.where(match, 1.0, 0.0).astype(BF)
    n, cols = first.shape[1], first.shape[2]
    row = lax.broadcasted_iota(jnp.int32, (2 * rank, cols), 0)
    col = lax.broadcasted_iota(jnp.int32, (2 * rank, cols), 1)
    copies[0].wait()
    held = None
    for m in range(2):
        take = (col == place[3] * rank + row - m * rank) & (row >= m * rank) & (row < (m + 1) * rank)
        term = dot(jnp.where(take, 1.0, 0.0).astype(BF), first_v[m], NT)
        held = term if held is None else held + term
    held = held.astype(BF)
    for j in range(2 * rank // extra):
        piece = held[j * extra : (j + 1) * extra, :]
        out[cap : cap + extra, j * n : (j + 1) * n] = piece
    far_copy = start(out.at[pl.ds(cap, extra), :], far_o, sems.at[3])
    copies[1].wait()
    out[:cap, :] = dot(pick, tokens_v[...]).astype(BF)
    copies[2].wait()
    out[cap + extra :, :] = (dot(pick, cotangent_v[...]) * gate).astype(BF)
    start(out, out_o, sems.at[4]).wait()
    far_copy.wait()


def expert_rows(tokens, cotangent, first, experts, values, rank, place):
    count, width = tokens.shape
    cap = count // 2
    extra = first.shape[1] * 2 * rank // width
    return call(
        functools.partial(rows_kernel, rank),
        [shape((2 * cap + extra, width)), shape((extra, width)), shape((cap, 1), F32)],
        [place, tokens, cotangent, first, experts, values],
        [SMEM, HBM, HBM, HBM, VMEM, VMEM],
        [HBM, HBM, VMEM],
        scratch=[
            pltpu.VMEM(tokens.shape, BF),
            pltpu.VMEM(cotangent.shape, BF),
            pltpu.VMEM(first.shape, BF),
            pltpu.VMEM((2 * cap + extra, width), BF),
            pltpu.SemaphoreType.DMA((5,)),
        ],
        name="expert_rows",
    )


N_Y = 4
CHUNK = 1024


def block_of(place, k, other):
    y, core = place[0], place[1]
    way = 1 - 2 * core
    return lax.rem(y + way * k + 2 * N_Y, N_Y) * 2 + (1 - core if other else core)


def wait(copies):
    for c in copies:
        c.wait()


def chunk_copies(i, outs, mine, other, sems):
    cols = pl.ds(pl.multiple_of(i * CHUNK, CHUNK), CHUNK)
    half = mine.shape[0]
    return [
        pltpu.make_async_copy(outs.at[pl.ds(half, half), cols], other.at[:, cols], sems.at[2 * i]),
        pltpu.make_async_copy(outs.at[pl.ds(0, half), cols], mine.at[:, cols], sems.at[2 * i + 1]),
    ]


def write_chunks(product, outs, mine, other, sems):
    def step(i, carry):
        product(pl.ds(pl.multiple_of(i * CHUNK, CHUNK), CHUNK))
        for c in chunk_copies(i, outs, mine, other, sems):
            c.start()
        return carry

    lax.fori_loop(0, outs.shape[1] // CHUNK, step, 0)


def finish_chunks(outs, mine, other, sems):
    def step(i, carry):
        wait(chunk_copies(i, outs, mine, other, sems))
        return carry

    lax.fori_loop(0, outs.shape[1] // CHUNK, step, 0)


def preactivations(xs, weights, second):
    h, rank = second.shape[2], second.shape[1]
    pre = dot(xs[...], weights[...], NT)
    low = pre[:, 2 * h :].astype(BF)
    gate = pre[:, :h] + ADAPTER_SCALE * dot(low[:, :rank], second[0])
    up = pre[:, h : 2 * h] + ADAPTER_SCALE * dot(low[:, rank:], second[1])
    return gate, up, low, (gate / (1.0 + jnp.exp(-gate)) * up).astype(BF)


def forward_kernel(cap, steps, place, *refs):
    n = 2 * len(steps)
    blocks, fars, (gate_up, down, second), refs = refs[:n], refs[n : n + 2], refs[n + 2 : n + 5], refs[n + 5 :]
    (gate_o, up_o, low_o, mine, other, first_out), refs = refs[:6], refs[6:]
    xs, weights, down_v, hidden, gate_v, up_v, low_v, packed, outs, in_sems, out_sems = refs
    h, rank, width = down.shape[0], second.shape[1], down.shape[1]
    lanes, extra = 2 * rank, fars[0].shape[0]
    first = weights.at[pl.ds(2 * h, lanes), :]
    count = iter(range(64))

    def fetch(source, target):
        return start(source, target, in_sems.at[next(count)])

    sources = [b.at[pl.ds(cap, extra), :] for b in blocks] + list(fars)
    got_first = [fetch(a, packed.at[pl.ds(i * extra, extra), :]) for i, a in enumerate(sources)]
    got_x = [fetch(b.at[pl.ds(0, cap), :], xs.at[pl.ds(i * cap, cap), :]) for i, b in enumerate(blocks)]
    got_gate_up = fetch(gate_up, weights.at[pl.ds(0, 2 * h), :])
    got_down = fetch(down, down_v)

    wait(got_first)
    step = extra * width // lanes
    held = [(k, o) for o in (False, True) for k in steps] + [(2, False), (2, True)]
    for i, (k, o) in enumerate(held):
        at = pl.ds(pl.multiple_of(block_of(place, k, o) * step, step), step)
        for j in range(lanes // extra):
            piece = packed[i * extra : (i + 1) * extra, j * step : (j + 1) * step]
            weights[2 * h + j * extra : 2 * h + (j + 1) * extra, at] = piece
    save = [start(first, first_out, out_sems.at[8])]
    wait(got_x)
    got_gate_up.wait()
    gate, up, low, act = preactivations(xs, weights, second)
    gate_v[...] = gate
    up_v[...] = up
    low_v[...] = low
    hidden[...] = act
    for i, (a, b) in enumerate(((gate_v, gate_o), (up_v, up_o), (low_v, low_o))):
        save.append(start(a, b, out_sems.at[9 + i]))
    got_down.wait()

    def product(cols):
        outs[:, cols] = dot(hidden[...], down_v[:, cols]).astype(BF)

    write_chunks(product, outs, mine, other, out_sems)
    finish_chunks(outs, mine, other, out_sems)
    wait(save)


def forward(cap, steps, place, blocks, fars, gate_up, down, second):
    n, width, h, both = len(blocks), down.shape[1], down.shape[0], 2 * second.shape[1]
    rows = n * cap
    return call(
        functools.partial(forward_kernel, cap, steps),
        [
            shape((rows, h), F32),
            shape((rows, h), F32),
            shape((rows, both)),
            shape((rows // 2, width)),
            shape((rows // 2, width)),
            shape((both, width)),
        ],
        [place, *blocks, *fars, gate_up, down, second],
        [SMEM] + [HBM] * (n + 4) + [VMEM],
        [HBM] * 6,
        scratch=[
            pltpu.VMEM((rows, width), BF),
            pltpu.VMEM((2 * h + both, width), BF),
            pltpu.VMEM(down.shape, BF),
            pltpu.VMEM((rows, h), BF),
            pltpu.VMEM((rows, h), F32),
            pltpu.VMEM((rows, h), F32),
            pltpu.VMEM((rows, both), BF),
            pltpu.VMEM(((n + 2) * fars[0].shape[0], width), BF),
            pltpu.VMEM((rows, width), BF),
            pltpu.SemaphoreType.DMA((2 * n + 4,)),
            pltpu.SemaphoreType.DMA((12,)),
        ],
        flops=10**10,
        name="forward_rows",
    )


def rest_kernel(cap, place, *refs):
    near, far_x, far_d, refs = refs[:6], refs[6:8], refs[8:10], refs[10:]
    (gate_n, up_n, low_n, gate_up, down, first, second), refs = refs[:7], refs[7:]
    (low_a, low_b, part, second_o, mine, other), refs = refs[:6], refs[6:]
    xs, ds, gate_v, up_v, low_v, weights, down_v, hidden, grads, outs, in_sems, out_sems = refs
    h, rank, width = down.shape[0], second.shape[1], down.shape[1]
    n = 2 * N_Y
    half = N_Y * cap
    count = iter(range(64))

    def fetch(source, target):
        return start(source, target, in_sems.at[next(count)])

    def rows_of(i):
        return pl.ds(i * cap, cap)

    place_of = {}
    for o in range(2):
        for j, k in enumerate((0, 1, 3)):
            place_of[o * N_Y + k] = (False, 3 * o + j)
        place_of[o * N_Y + 2] = (True, o)
    last = near[0].shape[0] - cap
    got_x = [fetch(far_x[o].at[pl.ds(0, cap), :], xs.at[rows_of(o), :]) for o in range(2)]
    got_weights = [fetch(gate_up, weights.at[pl.ds(0, 2 * h), :]), fetch(first, weights.at[pl.ds(2 * h, 2 * rank), :])]
    got_down = fetch(down, down_v)
    got_d, got_pre, saved = [], [], []
    for i in range(n):
        is_far, j = place_of[i]
        got_d.append(fetch(far_d[j] if is_far else near[j].at[pl.ds(last, cap), :], ds.at[rows_of(i), :]))
    for i in range(n):
        is_far, j = place_of[i]
        if not is_far:
            for source, target in ((gate_n, gate_v), (up_n, up_v), (low_n, low_v)):
                got_pre.append(fetch(source.at[rows_of(j), :], target.at[rows_of(i), :]))
    step = part.shape[1]
    cols = pl.ds(pl.multiple_of((place[0] * 2 + place[1]) * step, step), step)
    for i in range(n):
        is_far, j = place_of[i]
        at = pl.multiple_of(block_of(place, i % N_Y, i >= N_Y) * cap, cap)
        source = (far_x if is_far else near)[j].at[pl.ds(0, cap), cols]
        saved.append(start(source, part.at[pl.ds(at, cap), :], out_sems.at[8 + i]))

    wait(got_x)
    wait(got_weights)
    gate, up, low, act = preactivations(xs, weights, second)
    hidden[...] = act
    for o in range(2):
        to = (o * N_Y + 2) * cap
        for value, target in ((gate, gate_v), (up, up_v), (low, low_v)):
            target[to : to + cap, :] = value[o * cap : (o + 1) * cap, :]

    got_down.wait()
    wait(got_d)
    grad = dot(ds[...], down_v[...], NT)
    wait(got_pre)
    gate, up = gate_v[...], up_v[...]
    sig = 1.0 / (1.0 + jnp.exp(-gate))
    grad_gate = (grad * up * sig * (1.0 + gate * (1.0 - sig))).astype(BF)
    grad_up = (grad * gate * sig).astype(BF)
    both = [ADAPTER_SCALE * dot(grad_gate, second[0], NT), ADAPTER_SCALE * dot(grad_up, second[1], NT)]
    grad_low = jnp.concatenate(both, axis=1).astype(BF)
    grads[...] = jnp.concatenate([grad_gate, grad_up, grad_low], axis=1)

    def product(cols):
        got = dot(hidden[...], down_v[:, cols]).astype(BF)
        back = dot(grads[...], weights[:, cols]).astype(BF)
        for o in range(2):
            base = o * (half + cap)
            outs[base : base + cap, cols] = got[o * cap : (o + 1) * cap, :]
            outs[base + cap : base + cap + half, cols] = back[o * half : (o + 1) * half, :]

    write_chunks(product, outs, mine, other, out_sems)
    second_o[0] = ADAPTER_SCALE * dot(low_v[:, :rank], grad_gate, TN)
    second_o[1] = ADAPTER_SCALE * dot(low_v[:, rank:], grad_up, TN)

    lanes = 2 * rank
    row = lax.broadcasted_iota(jnp.int32, (lanes, lanes), 0)
    col = lax.broadcasted_iota(jnp.int32, (lanes, lanes), 1)
    members = rank // 4
    away, factor, member = row // (2 * members), (row // members) % 2, row % members
    wanted = factor * rank + (place[2] ^ away) * members + member
    order = jnp.where(wanted == col, 1.0, 0.0).astype(BF)
    straight = place[1] == 0
    for k in range(N_Y):
        ours = grad_low[k * cap : (k + 1) * cap, :].astype(F32)
        theirs = grad_low[(N_Y + k) * cap : (N_Y + k + 1) * cap, :].astype(F32)
        rows = jnp.concatenate([jnp.where(straight, ours, theirs), jnp.where(straight, theirs, ours)], axis=0)
        turned = dot(order, rows.astype(BF), NT).astype(BF)
        at = pl.multiple_of(lax.div(block_of(place, k, False), 2) * 2 * cap, 2 * cap)
        low_a[:, pl.ds(at, 2 * cap)] = turned[: lanes // 2, :]
        low_b[:, pl.ds(at, 2 * cap)] = turned[lanes // 2 :, :]
    finish_chunks(outs, mine, other, out_sems)
    wait(saved)


def rest(cap, place, near, far_x, far_d, pre_near, gate_up, down, first, second):
    width, h, both = down.shape[1], down.shape[0], 2 * second.shape[1]
    rows = 2 * N_Y * cap
    return call(
        functools.partial(rest_kernel, cap),
        [
            shape((both // 2, rows)),
            shape((both // 2, rows)),
            shape((rows, width // (2 * N_Y))),
            shape(second.shape, F32),
            shape((rows // 2 + cap, width)),
            shape((rows // 2 + cap, width)),
        ],
        [place, *near, *far_x, *far_d, *pre_near, gate_up, down, first, second],
        [SMEM] + [HBM] * 16 + [VMEM],
        [VMEM, VMEM, HBM, VMEM, HBM, HBM],
        scratch=[
            pltpu.VMEM((2 * cap, width), BF),
            pltpu.VMEM((rows, width), BF),
            pltpu.VMEM((rows, h), F32),
            pltpu.VMEM((rows, h), F32),
            pltpu.VMEM((rows, both), BF),
            pltpu.VMEM((2 * h + both, width), BF),
            pltpu.VMEM(down.shape, BF),
            pltpu.VMEM((2 * cap, h), BF),
            pltpu.VMEM((rows, 2 * h + both), BF),
            pltpu.VMEM((rows + 2 * cap, width), BF),
            pltpu.SemaphoreType.DMA((8 * N_Y + 3,)),
            pltpu.SemaphoreType.DMA((8 + 2 * N_Y,)),
        ],
        flops=10**10,
        name="rest_rows",
    )


def pack_kernel(cap, n_z, place, *refs):
    sources, outs, (own, came, packed, sems, out_sems) = refs[:4], refs[4 : 4 + 2 * N_Y], refs[4 + 2 * N_Y :]
    n = N_Y
    core, x = place[1], place[2]
    lanes = own.shape[2] // (n_z * n)
    copies = []
    for which in range(2):
        for k in range(n):
            for i, target in enumerate((own, came)):
                near, last = sources[2 * i], sources[2 * i + 1]
                if which:
                    source = last.at[pl.ds((1 + k) * cap, cap), :]
                elif k == 2:
                    source = last.at[pl.ds(0, cap), :]
                else:
                    source = near.at[pl.ds(min(k, 2) * cap, cap), :]
                to = target.at[which, pl.ds(k * cap, cap), :]
                copies.append(start(source, to, sems.at[len(copies)]))

    def block(which, i, q, z):
        cols = pl.ds(pl.multiple_of(z * n * lanes + lax.rem(x + q, n) * lanes, lanes), lanes)
        here = own[which, i * cap : (i + 1) * cap, cols].astype(F32)
        j = (n - i) % n
        return (here + came[which, j * cap : (j + 1) * cap, cols].astype(F32)).astype(BF)

    def store(which, straight):
        for to in range(n):
            for slot in range(n):
                i, q = (to, slot) if straight else (slot, to)
                for z in range(n_z):
                    rows, cols = slice(slot * cap, (slot + 1) * cap), slice(z * lanes, (z + 1) * lanes)
                    packed[which * n + to, rows, cols] = block(which, i, q, z)
            start(packed.at[which * n + to], outs[which * n + to], out_sems.at[which * n + to])

    for which in range(2):
        wait(copies[which * 2 * n : (which + 1) * 2 * n])

        @pl.when(core == 0)
        def _():
            store(which, True)

        @pl.when(core == 1)
        def _():
            store(which, False)

    for to in range(2 * n):
        pltpu.make_async_copy(packed.at[to], outs[to], out_sems.at[to]).wait()


def add_and_pack(cap, sources, place):
    n, n_z = N_Y, lax.axis_size("z")
    width = sources[0].shape[1]
    parts = call(
        functools.partial(pack_kernel, cap, n_z),
        [shape((n * cap, width // n))] * (2 * n),
        [place, *sources],
        [SMEM] + [HBM] * len(sources),
        [HBM] * (2 * n),
        scratch=[pltpu.VMEM((2, n * cap, width), BF)] * 2
        + [
            pltpu.VMEM((2 * n, n * cap, width // n), BF),
            pltpu.SemaphoreType.DMA((4 * n,)),
            pltpu.SemaphoreType.DMA((2 * n,)),
        ],
        limit=20,
        name="add_and_pack",
    )
    return parts[:n], parts[n:]


def total(parts):
    out = parts[0].astype(F32)
    for part in parts[1:]:
        out = out + part.astype(F32)
    return out


def first_moves(parts):
    return [parts[0]] + [crossed(parts[s], s, 0) for s in range(1, len(parts))]


def second_moves(once, n):
    cap = once.shape[0] // n
    blocks = [once[s * cap : (s + 1) * cap] for s in range(n)]
    return [blocks[0]] + [crossed(blocks[s], s, 1) for s in range(1, n)]


def to_tokens(rows, combine):
    n_z = lax.axis_size("z")
    cap = rows[0].shape[0]
    lanes = rows[0].shape[1] // n_z
    sent = [r.astype(BF).reshape(cap, n_z, lanes).transpose(1, 0, 2) for r in rows]
    came = lax.all_to_all(jnp.concatenate(sent, axis=2), "z", 0, 0, tiled=True)
    came = came.reshape(n_z * cap, len(rows) * lanes)
    sums = dot(combine, came).astype(BF)
    return [sums[:, i * lanes : (i + 1) * lanes] for i in range(len(rows))]


def shards(
    tokens,
    routed_experts,
    choice_weights,
    gate_up_weight,
    down_weight,
    adapter_first_factors,
    adapter_second_factors,
    cotangent,
):
    n_y, n_c, n_z, n_x = (lax.axis_size(a) for a in ("y", "core", "z", "x"))
    y, core, z, x = (lax.axis_index(a) for a in ("y", "core", "z", "x"))
    tok_count, width = tokens.shape
    cap = tok_count // 2
    rank = adapter_second_factors.shape[1]
    member_cols = rank // n_x
    hidden_count = down_weight.shape[0]
    part_width = width // (n_y * n_c)
    gate_up = gate_up_weight.swapaxes(1, 2).reshape(2 * hidden_count, width)

    place = jnp.stack([y, core, x, z]).astype(jnp.int32)
    own, far_first, row_gate = expert_rows(
        tokens, cotangent, adapter_first_factors, routed_experts.T, choice_weights.T, rank, place
    )
    chosen = jnp.any(routed_experts[:, :, None] == jnp.arange(n_z, dtype=jnp.int32), axis=1)
    earlier = jnp.arange(tok_count)[:, None] > jnp.arange(tok_count)[None, :]
    placed = dot(earlier.astype(BF), chosen.astype(BF)).astype(jnp.int32)
    combine = (placed[:, :, None] == jnp.arange(cap, dtype=jnp.int32)) & chosen[:, :, None]
    combine = combine.astype(BF).reshape(tok_count, n_z * cap)

    behind = ahead(own)
    front = ahead(own, -1)
    own_s = swap(own)
    far_first = ahead(far_first, 2)
    front_s = swap(behind)
    behind_s = swap(front)
    far_first_s = swap(far_first)
    relayed = tie(behind, front_s, behind_s, far_first_s)
    far_x = ahead(relayed[: own.shape[0] - cap])
    far_d = ahead(relayed[own.shape[0] - cap :])

    weights = (gate_up, down_weight)
    near = [own, front, behind, own_s, front_s, behind_s]
    *pre_near, mine_near, other_near, first = forward(
        cap, (0, 1, 3), place, near, [far_first, far_first_s], *weights, adapter_second_factors
    )
    came_near = swap(other_near)
    far_x, far_d, _ = lax.optimization_barrier((far_x, far_d, mine_near))
    far_x_s = swap(far_x)
    far_d_s = swap(far_d)
    low_a, low_b, x_part, second_gradient, mine_rest, other_rest = rest(
        cap, place, near, [far_x, far_x_s], [far_d, far_d_s], pre_near, *weights, first, adapter_second_factors
    )
    came_rest = swap(other_rest)

    def crossing(axis, bit):
        return [(i, i ^ bit) for i in range(lax.axis_size(axis))]

    cols = low_a.shape[0] // 2
    pair = low_a.astype(F32) + lax.ppermute(low_b, "x", crossing("x", 2)).astype(F32)
    low_sum = pair[:cols] + lax.ppermute(pair[cols:].astype(BF), "x", crossing("x", 1)).astype(F32)
    out_parts, in_parts = add_and_pack(cap, [mine_near, mine_rest, came_near, came_rest], place)
    out_got = first_moves(out_parts)
    in_got = first_moves(in_parts)
    out_once = total(out_got).astype(BF)
    mixed_rows = total(second_moves(out_once, n_y)) * row_gate
    low_sum = low_sum + swap(tie(low_sum, *in_got))
    in_once = tie(total(in_got).astype(BF), low_sum)
    in_moved = second_moves(in_once, n_y)
    low_sum = tie(low_sum, in_moved[1])
    low_sum = low_sum + lax.ppermute(low_sum, "y", crossing("y", 2))
    in_rows = tie(total(in_moved), low_sum)
    mixed, token_gradient = to_tokens([mixed_rows, in_rows], combine)
    summed = (low_sum + lax.ppermute(low_sum, "y", crossing("y", 1))).astype(BF)
    first_gradient = dot(summed, x_part).reshape(2, member_cols, part_width).transpose(0, 2, 1)
    return (mixed, token_gradient, first_gradient, second_gradient)


def solution(mesh):
    n_y, n_x = 4, 4
    n_dp, n_et = mesh.devices.shape
    fine = Mesh(
        mesh.devices.reshape(n_y, n_dp // n_y, n_et // n_x, n_x), ("y", "core", "z", "x")
    )
    dp, et = ("y", "core"), ("z", "x")
    both = et + dp
    return jax.shard_map(
        shards,
        mesh=fine,
        in_specs=(
            P(dp, None),
            P(dp, None),
            P(dp, None),
            P(None, None, both),
            P(both, None),
            P(None, dp, None),
            P(None, None, both),
            P(dp, None),
        ),
        out_specs=(P(dp, et), P(dp, et), P(None, dp, et), P(None, None, both)),
        check_vma=False,
    )
```

profile of v0, /device:TPU:8, one launch (start us, length us, event | category | flops | bytes accessed | tf_op | source)
XLA Modules:
  0.0 170.7 jit_solution(11125163137095190739)
XLA Ops:
  1.3 4.7 %expert_rows.1 = (bf16[144,4096]{1,0:T(8,128)(2,1)}, bf16[16,4096]{1,0:T(8,128)(2,1)}, f32[64,1]{1,0:T(8,128)}) custom-call(s32[4]{0:T(128)} %pad_add_fusion.place, bf16[128,4096]{1,0:T(8,128)(2,1)} %tokens.1, bf16[128,4096]{1,0:T(8,128)(2,1)} %cotangent.1, bf16[2,512,512]{2,1,0:T(8,128)(2,1)} %first.1, s32[2,128]{1,0:T(2,128)} %bitcast.36, f32[2,128]{1,0:T(2,128)} %bitcast.37), custom_call_target="tpu_custom_call" | custom-call | tf_op jit(solution)/shard_map/expert_rows/pallas_call | solution.py:32
  6.0 1.7 collective-permute-start.1
  8.3 26.8 %collective-permute-done.1.refs_2_ = bf16[144,4096]{1,0:T(8,128)(2,1)S(1)} collective-permute-done((bf16[144,4096]{1,0:T(8,128)(2,1)}, bf16[144,4096]{1,0:T(8,128)(2,1)S(1)}, u32[]{:S(2)}, u32[]{:S(2)}) %collective-permute-start.1) | collective-permute-done | bytes 1179680 | tf_op jit(solution)/shard_map/ppermute | solution.py:61
  35.7 2.3 %collective-permute-start.5 = (bf16[16,4096]{1,0:T(8,128)(2,1)}, bf16[16,4096]{1,0:T(8,128)(2,1)S(1)}, u32[]{:S(2)}, u32[]{:S(2)}) collective-permute-start(bf16[16,4096]{1,0:T(8,128)(2,1)} %get-tuple-element.35), channel_id=1, source_target_pairs={{0,128},{32,160},{64,192},{96,224},{128,0},{160,32},{192,64},{224,... | collective-permute-start | bytes 393224 | tf_op jit(solution)/shard_map/ppermute | solution.py:61
  38.0 5.3 %collective-permute-done.5.refs_6_ = bf16[16,4096]{1,0:T(8,128)(2,1)S(1)} collective-permute-done((bf16[16,4096]{1,0:T(8,128)(2,1)}, bf16[16,4096]{1,0:T(8,128)(2,1)S(1)}, u32[]{:S(2)}, u32[]{:S(2)}) %collective-permute-start.5) | collective-permute-done | bytes 131104 | tf_op jit(solution)/shard_map/ppermute | solution.py:61
  43.2 1.3 collective-permute-done.6.refs_7_
  45.8 1.6 collective-permute-start.8
  48.3 12.9 %forward_rows.1 = (f32[384,336]{1,0:T(8,128)}, f32[384,336]{1,0:T(8,128)}, bf16[384,128]{1,0:T(8,128)(2,1)}, bf16[192,4096]{1,0:T(8,128)(2,1)}, bf16[192,4096]{1,0:T(8,128)(2,1)}, /*index=5*/bf16[128,4096]{1,0:T(8,128)(2,1)}) custom-call(s32[4]{0:T(128)} %pad_add_fusion.place, bf16[144,4096]{1,0:T(8,128)(2,1)} %get-tuple-element.34.refs_0_, ...), custom_call_target="tpu_custom_call" | custom-call | flops 10000000000 | tf_op jit(solution)/shard_map/forward_rows/pallas_call | solution.py:32
  61.2 2.2 %collective-permute-done.7.refs_6_ = bf16[80,4096]{1,0:T(8,128)(2,1)} collective-permute-done((bf16[80,4096]{1,0:T(8,128)(2,1)S(1)}, bf16[80,4096]{1,0:T(8,128)(2,1)}, u32[]{:S(2)}, u32[]{:S(2)}) %collective-permute-start.7) | collective-permute-done | bytes 655392 | tf_op jit(solution)/shard_map/ppermute | solution.py:61
  63.9 2.5 %collective-permute-done.10.refs_9_ = bf16[64,4096]{1,0:T(8,128)(2,1)S(1)} collective-permute-done((bf16[64,4096]{1,0:T(8,128)(2,1)}, bf16[64,4096]{1,0:T(8,128)(2,1)S(1)}, u32[]{:S(2)}, u32[]{:S(2)}) %collective-permute-start.10) | collective-permute-done | bytes 524320 | tf_op jit(solution)/shard_map/ppermute | solution.py:55
  67.5 19.2 %rest_rows.1 = (bf16[64,512]{1,0:T(8,128)(2,1)}, bf16[64,512]{1,0:T(8,128)(2,1)}, bf16[512,512]{1,0:T(8,128)(2,1)}, f32[2,64,336]{2,1,0:T(8,128)}, bf16[320,4096]{1,0:T(8,128)(2,1)}, /*index=5*/bf16[320,4096]{1,0:T(8,128)(2,1)}) custom-call(s32[4]{0:T(128)} %pad_add_fusion.place, bf16[144,4096]{1,0:T(8,128)(2,1)} %get-tuple-element.34.refs_0_, ...), custom_call_target="tpu_custom_call" | custom-call | flops 10000000000 | tf_op jit(solution)/shard_map/rest_rows/pallas_call | solution.py:32
  87.4 1.4 collective-permute-start.22
  88.8 5.4 %collective-permute-done.11.refs_2_ = bf16[192,4096]{1,0:T(8,128)(2,1)S(1)} collective-permute-done((bf16[192,4096]{1,0:T(8,128)(2,1)}, bf16[192,4096]{1,0:T(8,128)(2,1)S(1)}, u32[]{:S(2)}, u32[]{:S(2)}) %collective-permute-start.11) | collective-permute-done | bytes 1572896 | tf_op jit(solution)/shard_map/ppermute | solution.py:55
  94.2 1.7 %copy-done = bf16[320,4096]{1,0:T(8,128)(2,1)S(1)} copy-done((bf16[320,4096]{1,0:T(8,128)(2,1)S(1)}, bf16[320,4096]{1,0:T(8,128)(2,1)}, u32[]{:S(2)}) %copy-start) | copy-done | bytes 2621464
  96.0 4.0 %add_and_pack.1 = (bf16[256,1024]{1,0:T(8,128)(2,1)S(1)}, bf16[256,1024]{1,0:T(8,128)(2,1)}, bf16[256,1024]{1,0:T(8,128)(2,1)}, bf16[256,1024]{1,0:T(8,128)(2,1)...) custom-call(s32[4]{0:T(128)S(1)} %copy-done.2, ...), custom_call_target="tpu_custom_call" | custom-call | tf_op jit(solution)/shard_map/add_and_pack/pallas_call | solution.py:32
  100.8 1.4 collective-permute-start.13
  102.1 3.9 %collective-permute-start.14 = (bf16[256,1024]{1,0:T(8,128)(2,1)}, bf16[256,1024]{1,0:T(8,128)(2,1)}, u32[]{:S(2)}, u32[]{:S(2)}) collective-permute-start(bf16[256,1024]{1,0:T(8,128)(2,1)} %get-tuple-element.49), channel_id=1, source_target_pairs={{0,128},{1,129},{2,130},{3,131},{32,34},{33,35},{34,32},{35,33},{6... | collective-permute-start | bytes 1572872 | tf_op jit(solution)/shard_map/ppermute | solution.py:72
  106.4 4.2 %collective-permute-done.23 = bf16[32,512]{1,0:T(8,128)(2,1)S(1)} collective-permute-done((bf16[32,512]{1,0:T(8,128)(2,1)S(1)}, bf16[32,512]{1,0:T(8,128)(2,1)S(1)}, u32[]{:S(2)}, u32[]{:S(2)}) %collective-permute-start.23) | collective-permute-done | bytes 32800 | tf_op jit(solution)/shard_map/ppermute | solution.py:559
  110.5 2.1 %collective-permute-start.19 = (bf16[256,1024]{1,0:T(8,128)(2,1)}, bf16[256,1024]{1,0:T(8,128)(2,1)S(1)}, u32[]{:S(2)}, u32[]{:S(2)}) collective-permute-start(bf16[256,1024]{1,0:T(8,128)(2,1)} %copy-done.3), channel_id=1, source_target_pairs={{0,64},{1,65},{2,66},{3,67},{32,33},{33,34},{34,35},{35,32},{64,12... | collective-permute-start | bytes 1572872 | tf_op jit(solution)/shard_map/ppermute | solution.py:72
  112.6 1.2 collective-permute-start.20
  113.9 6.4 %collective-permute-start.21 = (bf16[256,1024]{1,0:T(8,128)(2,1)S(1)}, bf16[256,1024]{1,0:T(8,128)(2,1)S(1)}, u32[]{:S(2)}, u32[]{:S(2)}) collective-permute-start(bf16[256,1024]{1,0:T(8,128)(2,1)S(1)} %get-tuple-element.55), channel_id=1, source_target_pairs={{0,192},{1,193},{2,194},{3,195},{32,35},{33,32},{34,33},{35,34},{6... | collective-permute-start | bytes 1572872 | tf_op jit(solution)/shard_map/ppermute | solution.py:72
  120.2 1.6 add_convert_fusion.1
  121.9 3.2 %collective-permute-start.18 = (bf16[64,1024]{1,0:T(8,128)(2,1)S(1)}, bf16[64,1024]{1,0:T(8,128)(2,1)S(1)}, u32[]{:S(2)}, u32[]{:S(2)}) collective-permute-start(bf16[64,1024]{1,0:T(8,128)(2,1)S(1)} %get-tuple-element.65), channel_id=1, source_target_pairs={{0,3},{1,0},{2,1},{3,2},{32,96},{33,97},{34,98},{35,99},{64,67},{6... | collective-permute-start | bytes 393224 | tf_op jit(solution)/shard_map/ppermute | solution.py:72
  125.2 6.5 %collective-permute-done.21 = bf16[256,1024]{1,0:T(8,128)(2,1)S(1)} collective-permute-done((bf16[256,1024]{1,0:T(8,128)(2,1)S(1)}, bf16[256,1024]{1,0:T(8,128)(2,1)S(1)}, u32[]{:S(2)}, u32[]{:S(2)}) %collective-permute-start.21) | collective-permute-done | bytes 524320 | tf_op jit(solution)/shard_map/ppermute | solution.py:72
  131.7 4.4 %collective-permute-start.24 = (f32[32,512]{1,0:T(8,128)S(1)}, f32[32,512]{1,0:T(8,128)S(1)}, u32[]{:S(2)}, u32[]{:S(2)}) collective-permute-start(f32[32,512]{1,0:T(8,128)S(1)} %slice_add_fusion), channel_id=1, source_target_pairs={{0,32},{32,0},{1,33},{33,1},{2,34},{34,2},{3,35},{35,3},{4,36},{36... | collective-permute-start | bytes 196616 | tf_op jit(solution)/shard_map/ppermute | solution.py:55
  137.9 2.5 %collective-permute-start.27 = (bf16[64,1024]{1,0:T(8,128)(2,1)S(1)}, bf16[64,1024]{1,0:T(8,128)(2,1)S(1)}, u32[]{:S(2)}, u32[]{:S(2)}) collective-permute-start(bf16[64,1024]{1,0:T(8,128)(2,1)S(1)} %get-tuple-element.68), channel_id=1, source_target_pairs={{0,3},{1,0},{2,1},{3,2},{32,96},{33,97},{34,98},{35,99},{64,67},{6... | collective-permute-start | bytes 393224 | tf_op jit(solution)/shard_map/ppermute | solution.py:72
  141.4 2.0 %collective-permute-done.25 = bf16[64,1024]{1,0:T(8,128)(2,1)S(1)} collective-permute-done((bf16[64,1024]{1,0:T(8,128)(2,1)S(1)}, bf16[64,1024]{1,0:T(8,128)(2,1)S(1)}, u32[]{:S(2)}, u32[]{:S(2)}) %collective-permute-start.25) | collective-permute-done | bytes 131104 | tf_op jit(solution)/shard_map/ppermute | solution.py:72
  143.3 2.6 %collective-permute-start.28 = (f32[32,512]{1,0:T(8,128)S(1)}, f32[32,512]{1,0:T(8,128)S(1)}, u32[]{:S(2)}, u32[]{:S(2)}) collective-permute-start(f32[32,512]{1,0:T(8,128)S(1)} %add.62), channel_id=1, source_target_pairs={{0,128},{64,192},{128,0},{192,64},{1,129},{65,193},{129,1},{193,65... | collective-permute-start | bytes 196616 | tf_op jit(solution)/shard_map/ppermute | solution.py:569
  146.9 2.2 %collective-permute-done.28 = f32[32,512]{1,0:T(8,128)S(1)} collective-permute-done((f32[32,512]{1,0:T(8,128)S(1)}, f32[32,512]{1,0:T(8,128)S(1)}, u32[]{:S(2)}, u32[]{:S(2)}) %collective-permute-start.28) | collective-permute-done | bytes 65568 | tf_op jit(solution)/shard_map/ppermute | solution.py:569
  149.1 3.4 %collective-permute-start.29 = (f32[32,512]{1,0:T(8,128)S(1)}, f32[32,512]{1,0:T(8,128)S(1)}, u32[]{:S(2)}, u32[]{:S(2)}) collective-permute-start(f32[32,512]{1,0:T(8,128)S(1)} %add.66), channel_id=1, source_target_pairs={{0,64},{64,0},{128,192},{192,128},{1,65},{65,1},{129,193},{193,129... | collective-permute-start | bytes 196616 | tf_op jit(solution)/shard_map/ppermute | solution.py:572
  153.3 6.0 %all-to-all-start = ((bf16[8,64,256]{2,1,0:T(8,128)(2,1)}), bf16[8,64,256]{2,1,0:T(8,128)(2,1)S(1)}, u32[]{:S(2)}, u32[]{:S(2)}) async-start(bf16[8,64,256]{2,1,0:T(8,128)(2,1)} %pad_maximum_fusion), calls=%async_computation | async-start | bytes 524288 | tf_op jit(solution)/shard_map/all_to_all | solution.py:493
  160.3 9.5 %all-to-all-done = bf16[8,64,256]{2,1,0:T(8,128)(2,1)S(1)} async-done(((bf16[8,64,256]{2,1,0:T(8,128)(2,1)}), bf16[8,64,256]{2,1,0:T(8,128)(2,1)S(1)}, u32[]{:S(2)}, u32[]{:S(2)}) %all-to-all-start) | async-done | bytes 262176 | tf_op jit(solution)/shard_map/all_to_all | solution.py:493
  (86 shorter events, 13.9 us)
Async XLA Ops:
  6.0 29.1 %collective-permute-start.1 = (bf16[144,4096]{1,0:T(8,128)(2,1)}, bf16[144,4096]{1,0:T(8,128)(2,1)S(1)}, u32[]{:S(2)}, u32[]{:S(2)}) collective-permute-start(bf16[144,4096]{1,0:T(8,128)(2,1)} %get-tuple-element.34.refs_0_), channel_id=1, source_target_pairs={{0,64},{32,224},{64,128},{96,32},{128,192},{160,96},{192,0},{224,1... | collective-permute-start | bytes 3538952 | tf_op jit(solution)/shard_map/ppermute | solution.py:61
  7.6 27.5 %collective-permute-start = (bf16[144,4096]{1,0:T(8,128)(2,1)}, bf16[144,4096]{1,0:T(8,128)(2,1)S(1)}, u32[]{:S(2)}, u32[]{:S(2)}) collective-permute-start(bf16[144,4096]{1,0:T(8,128)(2,1)} %get-tuple-element.34.refs_0_), channel_id=1, source_target_pairs={{0,192},{32,96},{64,0},{96,160},{128,64},{160,224},{192,128},{224,... | collective-permute-start | bytes 3538952 | tf_op jit(solution)/shard_map/ppermute | solution.py:61
  35.1 9.5 %collective-permute-start.3 = (bf16[144,4096]{1,0:T(8,128)(2,1)S(1)}, bf16[144,4096]{1,0:T(8,128)(2,1)S(1)}, u32[]{:S(2)}, u32[]{:S(2)}) collective-permute-start(bf16[144,4096]{1,0:T(8,128)(2,1)S(1)} %collective-permute-done.1.refs_2_), channel_id=1, source_target_pairs={{0,32},{32,0},{1,33},{33,1},{2,34},{34,2},{3,35},{35,3},{4,36},{36... | collective-permute-start | bytes 3538952 | tf_op jit(solution)/shard_map/ppermute | solution.py:55
  35.1 10.6 %collective-permute-start.4 = (bf16[144,4096]{1,0:T(8,128)(2,1)S(1)}, bf16[144,4096]{1,0:T(8,128)(2,1)}, u32[]{:S(2)}, u32[]{:S(2)}) collective-permute-start(bf16[144,4096]{1,0:T(8,128)(2,1)S(1)} %collective-permute-done.refs_1_), channel_id=1, source_target_pairs={{0,32},{32,0},{1,33},{33,1},{2,34},{34,2},{3,35},{35,3},{4,36},{36... | collective-permute-start | bytes 3538952 | tf_op jit(solution)/shard_map/ppermute | solution.py:55
  35.6 12.7 %collective-permute-start.2 = (bf16[144,4096]{1,0:T(8,128)(2,1)}, bf16[144,4096]{1,0:T(8,128)(2,1)}, u32[]{:S(2)}, u32[]{:S(2)}) collective-permute-start(bf16[144,4096]{1,0:T(8,128)(2,1)} %get-tuple-element.34.refs_0_), channel_id=1, source_target_pairs={{0,32},{32,0},{1,33},{33,1},{2,34},{34,2},{3,35},{35,3},{4,36},{36... | collective-permute-start | bytes 3538952 | tf_op jit(solution)/shard_map/ppermute | solution.py:55
  35.7 7.5 %collective-permute-start.5 = (bf16[16,4096]{1,0:T(8,128)(2,1)}, bf16[16,4096]{1,0:T(8,128)(2,1)S(1)}, u32[]{:S(2)}, u32[]{:S(2)}) collective-permute-start(bf16[16,4096]{1,0:T(8,128)(2,1)} %get-tuple-element.35), channel_id=1, source_target_pairs={{0,128},{32,160},{64,192},{96,224},{128,0},{160,32},{192,64},{224,... | collective-permute-start | bytes 393224 | tf_op jit(solution)/shard_map/ppermute | solution.py:61
  43.2 1.3 collective-permute-start.6
  45.8 15.4 %collective-permute-start.8 = (bf16[64,4096]{1,0:T(8,128)(2,1)S(1)}, bf16[64,4096]{1,0:T(8,128)(2,1)}, u32[]{:S(2)}, u32[]{:S(2)}) collective-permute-start(bf16[64,4096]{1,0:T(8,128)(2,1)S(1)} %slice.44), channel_id=1, source_target_pairs={{0,64},{32,224},{64,128},{96,32},{128,192},{160,96},{192,0},{224,1... | collective-permute-start | bytes 1572872 | tf_op jit(solution)/shard_map/ppermute | solution.py:61
  47.3 16.1 %collective-permute-start.7 = (bf16[80,4096]{1,0:T(8,128)(2,1)S(1)}, bf16[80,4096]{1,0:T(8,128)(2,1)}, u32[]{:S(2)}, u32[]{:S(2)}) collective-permute-start(bf16[80,4096]{1,0:T(8,128)(2,1)S(1)} %slice.43), channel_id=1, source_target_pairs={{0,64},{32,224},{64,128},{96,32},{128,192},{160,96},{192,0},{224,1... | collective-permute-start | bytes 1966088 | tf_op jit(solution)/shard_map/ppermute | solution.py:61
  63.4 3.1 %collective-permute-start.9 = (bf16[80,4096]{1,0:T(8,128)(2,1)}, bf16[80,4096]{1,0:T(8,128)(2,1)S(1)}, u32[]{:S(2)}, u32[]{:S(2)}) collective-permute-start(bf16[80,4096]{1,0:T(8,128)(2,1)} %collective-permute-done.7.refs_6_), channel_id=1, source_target_pairs={{0,32},{32,0},{1,33},{33,1},{2,34},{34,2},{3,35},{35,3},{4,36},{36... | collective-permute-start | bytes 1966088 | tf_op jit(solution)/shard_map/ppermute | solution.py:55
  63.4 3.1 %collective-permute-start.10 = (bf16[64,4096]{1,0:T(8,128)(2,1)}, bf16[64,4096]{1,0:T(8,128)(2,1)S(1)}, u32[]{:S(2)}, u32[]{:S(2)}) collective-permute-start(bf16[64,4096]{1,0:T(8,128)(2,1)} %collective-permute-done.8.refs_8_), channel_id=1, source_target_pairs={{0,32},{32,0},{1,33},{33,1},{2,34},{34,2},{3,35},{35,3},{4,36},{36... | collective-permute-start | bytes 1572872 | tf_op jit(solution)/shard_map/ppermute | solution.py:55
  67.5 26.7 %copy-start.2 = (s32[4]{0:T(128)S(1)}, s32[4]{0:T(128)}, u32[]{:S(2)}) copy-start(s32[4]{0:T(128)} %pad_add_fusion.place) | copy-start | bytes 52
  86.8 7.5 %collective-permute-start.12 = (bf16[320,4096]{1,0:T(8,128)(2,1)}, bf16[320,4096]{1,0:T(8,128)(2,1)S(1)}, u32[]{:S(2)}, u32[]{:S(2)}) collective-permute-start(bf16[320,4096]{1,0:T(8,128)(2,1)} %get-tuple-element.46), channel_id=1, source_target_pairs={{0,32},{32,0},{1,33},{33,1},{2,34},{34,2},{3,35},{35,3},{4,36},{36... | collective-permute-start | bytes 7864328 | tf_op jit(solution)/shard_map/ppermute | solution.py:55
  87.0 7.2 %collective-permute-start.11 = (bf16[192,4096]{1,0:T(8,128)(2,1)}, bf16[192,4096]{1,0:T(8,128)(2,1)S(1)}, u32[]{:S(2)}, u32[]{:S(2)}) collective-permute-start(bf16[192,4096]{1,0:T(8,128)(2,1)} %get-tuple-element.45), channel_id=1, source_target_pairs={{0,32},{32,0},{1,33},{33,1},{2,34},{34,2},{3,35},{35,3},{4,36},{36... | collective-permute-start | bytes 4718600 | tf_op jit(solution)/shard_map/ppermute | solution.py:55
  87.4 18.7 %collective-permute-start.22 = (bf16[64,512]{1,0:T(8,128)(2,1)}, bf16[64,512]{1,0:T(8,128)(2,1)S(1)}, u32[]{:S(2)}, u32[]{:S(2)}) collective-permute-start(bf16[64,512]{1,0:T(8,128)(2,1)} %get-tuple-element.57), channel_id=1, source_target_pairs={{0,2},{1,3},{2,0},{3,1},{4,6},{5,7},{6,4},{7,5},{8,10},{9,11},{10,... | collective-permute-start | bytes 196616 | tf_op jit(solution)/shard_map/ppermute | solution.py:558
  100.8 13.1 %collective-permute-start.13 = (bf16[256,1024]{1,0:T(8,128)(2,1)}, bf16[256,1024]{1,0:T(8,128)(2,1)S(1)}, u32[]{:S(2)}, u32[]{:S(2)}) collective-permute-start(bf16[256,1024]{1,0:T(8,128)(2,1)} %get-tuple-element.48), channel_id=1, source_target_pairs={{0,64},{1,65},{2,66},{3,67},{32,33},{33,34},{34,35},{35,32},{64,12... | collective-permute-start | bytes 1572872 | tf_op jit(solution)/shard_map/ppermute | solution.py:72
  102.1 18.1 %collective-permute-start.14 = (bf16[256,1024]{1,0:T(8,128)(2,1)}, bf16[256,1024]{1,0:T(8,128)(2,1)}, u32[]{:S(2)}, u32[]{:S(2)}) collective-permute-start(bf16[256,1024]{1,0:T(8,128)(2,1)} %get-tuple-element.49), channel_id=1, source_target_pairs={{0,128},{1,129},{2,130},{3,131},{32,34},{33,35},{34,32},{35,33},{6... | collective-permute-start | bytes 1572872 | tf_op jit(solution)/shard_map/ppermute | solution.py:72
  106.1 14.2 %collective-permute-start.15 = (bf16[256,1024]{1,0:T(8,128)(2,1)}, bf16[256,1024]{1,0:T(8,128)(2,1)}, u32[]{:S(2)}, u32[]{:S(2)}) collective-permute-start(bf16[256,1024]{1,0:T(8,128)(2,1)} %get-tuple-element.50), channel_id=1, source_target_pairs={{0,192},{1,193},{2,194},{3,195},{32,35},{33,32},{34,33},{35,34},{6... | collective-permute-start | bytes 1572872 | tf_op jit(solution)/shard_map/ppermute | solution.py:72
  106.1 4.4 %collective-permute-start.23 = (bf16[32,512]{1,0:T(8,128)(2,1)S(1)}, bf16[32,512]{1,0:T(8,128)(2,1)S(1)}, u32[]{:S(2)}, u32[]{:S(2)}) collective-permute-start(bf16[32,512]{1,0:T(8,128)(2,1)S(1)} %slice.69), channel_id=1, source_target_pairs={{0,1},{1,0},{2,3},{3,2},{4,5},{5,4},{6,7},{7,6},{8,9},{9,8},{10,11... | collective-permute-start | bytes 98312 | tf_op jit(solution)/shard_map/ppermute | solution.py:559
  110.5 14.6 %collective-permute-start.19 = (bf16[256,1024]{1,0:T(8,128)(2,1)}, bf16[256,1024]{1,0:T(8,128)(2,1)S(1)}, u32[]{:S(2)}, u32[]{:S(2)}) collective-permute-start(bf16[256,1024]{1,0:T(8,128)(2,1)} %copy-done.3), channel_id=1, source_target_pairs={{0,64},{1,65},{2,66},{3,67},{32,33},{33,34},{34,35},{35,32},{64,12... | collective-permute-start | bytes 1572872 | tf_op jit(solution)/shard_map/ppermute | solution.py:72
  112.6 12.5 %collective-permute-start.20 = (bf16[256,1024]{1,0:T(8,128)(2,1)S(1)}, bf16[256,1024]{1,0:T(8,128)(2,1)S(1)}, u32[]{:S(2)}, u32[]{:S(2)}) collective-permute-start(bf16[256,1024]{1,0:T(8,128)(2,1)S(1)} %get-tuple-element.54), channel_id=1, source_target_pairs={{0,128},{1,129},{2,130},{3,131},{32,34},{33,35},{34,32},{35,33},{6... | collective-permute-start | bytes 1572872 | tf_op jit(solution)/shard_map/ppermute | solution.py:72
  113.9 17.8 %collective-permute-start.21 = (bf16[256,1024]{1,0:T(8,128)(2,1)S(1)}, bf16[256,1024]{1,0:T(8,128)(2,1)S(1)}, u32[]{:S(2)}, u32[]{:S(2)}) collective-permute-start(bf16[256,1024]{1,0:T(8,128)(2,1)S(1)} %get-tuple-element.55), channel_id=1, source_target_pairs={{0,192},{1,193},{2,194},{3,195},{32,35},{33,32},{34,33},{35,34},{6... | collective-permute-start | bytes 1572872 | tf_op jit(solution)/shard_map/ppermute | solution.py:72
  121.8 18.6 %collective-permute-start.16 = (bf16[64,1024]{1,0:T(8,128)(2,1)S(1)}, bf16[64,1024]{1,0:T(8,128)(2,1)S(1)}, u32[]{:S(2)}, u32[]{:S(2)}) collective-permute-start(bf16[64,1024]{1,0:T(8,128)(2,1)S(1)} %get-tuple-element.64), channel_id=1, source_target_pairs={{0,1},{1,2},{2,3},{3,0},{32,224},{33,225},{34,226},{35,227},{64,65... | collective-permute-start | bytes 393224 | tf_op jit(solution)/shard_map/ppermute | solution.py:72
  121.9 19.3 %collective-permute-start.18 = (bf16[64,1024]{1,0:T(8,128)(2,1)S(1)}, bf16[64,1024]{1,0:T(8,128)(2,1)S(1)}, u32[]{:S(2)}, u32[]{:S(2)}) collective-permute-start(bf16[64,1024]{1,0:T(8,128)(2,1)S(1)} %get-tuple-element.65), channel_id=1, source_target_pairs={{0,3},{1,0},{2,1},{3,2},{32,96},{33,97},{34,98},{35,99},{64,67},{6... | collective-permute-start | bytes 393224 | tf_op jit(solution)/shard_map/ppermute | solution.py:72
  125.1 16.1 %collective-permute-start.17 = (bf16[64,1024]{1,0:T(8,128)(2,1)S(1)}, bf16[64,1024]{1,0:T(8,128)(2,1)S(1)}, u32[]{:S(2)}, u32[]{:S(2)}) collective-permute-start(bf16[64,1024]{1,0:T(8,128)(2,1)S(1)} %get-tuple-element.66), channel_id=1, source_target_pairs={{0,2},{1,3},{2,0},{3,1},{32,160},{33,161},{34,162},{35,163},{64,66... | collective-permute-start | bytes 393224 | tf_op jit(solution)/shard_map/ppermute | solution.py:72
  131.7 5.3 %collective-permute-start.24 = (f32[32,512]{1,0:T(8,128)S(1)}, f32[32,512]{1,0:T(8,128)S(1)}, u32[]{:S(2)}, u32[]{:S(2)}) collective-permute-start(f32[32,512]{1,0:T(8,128)S(1)} %slice_add_fusion), channel_id=1, source_target_pairs={{0,32},{32,0},{1,33},{33,1},{2,34},{34,2},{3,35},{35,3},{4,36},{36... | collective-permute-start | bytes 196616 | tf_op jit(solution)/shard_map/ppermute | solution.py:55
  137.1 6.3 %collective-permute-start.25 = (bf16[64,1024]{1,0:T(8,128)(2,1)S(1)}, bf16[64,1024]{1,0:T(8,128)(2,1)S(1)}, u32[]{:S(2)}, u32[]{:S(2)}) collective-permute-start(bf16[64,1024]{1,0:T(8,128)(2,1)S(1)} %get-tuple-element.67), channel_id=1, source_target_pairs={{0,1},{1,2},{2,3},{3,0},{32,224},{33,225},{34,226},{35,227},{64,65... | collective-permute-start | bytes 393224 | tf_op jit(solution)/shard_map/ppermute | solution.py:72
  137.9 8.0 %collective-permute-start.27 = (bf16[64,1024]{1,0:T(8,128)(2,1)S(1)}, bf16[64,1024]{1,0:T(8,128)(2,1)S(1)}, u32[]{:S(2)}, u32[]{:S(2)}) collective-permute-start(bf16[64,1024]{1,0:T(8,128)(2,1)S(1)} %get-tuple-element.68), channel_id=1, source_target_pairs={{0,3},{1,0},{2,1},{3,2},{32,96},{33,97},{34,98},{35,99},{64,67},{6... | collective-permute-start | bytes 393224 | tf_op jit(solution)/shard_map/ppermute | solution.py:72
  140.4 6.5 %collective-permute-start.26 = (bf16[64,1024]{1,0:T(8,128)(2,1)S(1)}, bf16[64,1024]{1,0:T(8,128)(2,1)S(1)}, u32[]{:S(2)}, u32[]{:S(2)}) collective-permute-start(bf16[64,1024]{1,0:T(8,128)(2,1)S(1)} %get-tuple-element.69), channel_id=1, source_target_pairs={{0,2},{1,3},{2,0},{3,1},{32,160},{33,161},{34,162},{35,163},{64,66... | collective-permute-start | bytes 393224 | tf_op jit(solution)/shard_map/ppermute | solution.py:72
  143.3 5.8 %collective-permute-start.28 = (f32[32,512]{1,0:T(8,128)S(1)}, f32[32,512]{1,0:T(8,128)S(1)}, u32[]{:S(2)}, u32[]{:S(2)}) collective-permute-start(f32[32,512]{1,0:T(8,128)S(1)} %add.62), channel_id=1, source_target_pairs={{0,128},{64,192},{128,0},{192,64},{1,129},{65,193},{129,1},{193,65... | collective-permute-start | bytes 196616 | tf_op jit(solution)/shard_map/ppermute | solution.py:569
  149.1 10.3 %collective-permute-start.29 = (f32[32,512]{1,0:T(8,128)S(1)}, f32[32,512]{1,0:T(8,128)S(1)}, u32[]{:S(2)}, u32[]{:S(2)}) collective-permute-start(f32[32,512]{1,0:T(8,128)S(1)} %add.66), channel_id=1, source_target_pairs={{0,64},{64,0},{128,192},{192,128},{1,65},{65,1},{129,193},{193,129... | collective-permute-start | bytes 196616 | tf_op jit(solution)/shard_map/ppermute | solution.py:572
  153.3 16.5 %all-to-all-start = ((bf16[8,64,256]{2,1,0:T(8,128)(2,1)}), bf16[8,64,256]{2,1,0:T(8,128)(2,1)S(1)}, u32[]{:S(2)}, u32[]{:S(2)}) async-start(bf16[8,64,256]{2,1,0:T(8,128)(2,1)} %pad_maximum_fusion), calls=%async_computation | async-start | bytes 524288 | tf_op jit(solution)/shard_map/all_to_all | solution.py:493
  (14 other events, 120.3 us)
where the time goes:
time: 171 us
  waiting for transfers between devices  69.5 us (41%)
  starting transfers between devices  49.2 us (29%)
  Pallas kernels  40.8 us (24%)
  local copies, waits for them, and re-layouts  5.48 us (3%)
  other arithmetic  3.63 us (2%)
    pallas_call x4, Pallas kernels, call(): pl.pallas_call(kernel, out_shape=out_shape, in_specs=in_specs, out_specs=...  40.8 us
    ppermute x5, waiting for transfers between devices, ahead(): return lax.ppermute(values, ('y', 'core'), pairs)  34.2 us
    ppermute x12, starting transfers between devices, crossed(): return lax.ppermute(values, ('y', 'core', 'x'), pairs)  22.4 us
    ppermute x9, waiting for transfers between devices, swap(): return lax.ppermute(values, 'core', [(0, 1), (1, 0)])  9.87 us
    ppermute x12, waiting for transfers between devices, crossed(): return lax.ppermute(values, ('y', 'core', 'x'), pairs)  9.51 us
    all_to_all x1, waiting for transfers between devices, to_tokens(): came = lax.all_to_all(jnp.concatenate(sent, axis=2), 'z', 0, 0, tiled=True)  9.49 us
    ppermute x5, starting transfers between devices, ahead(): return lax.ppermute(values, ('y', 'core'), pairs)  7.14 us
    ppermute x9, starting transfers between devices, swap(): return lax.ppermute(values, 'core', [(0, 1), (1, 0)])  6.12 us
  transfers between devices with their start and end apart: 31, of which 13 were waited for; matrix products, arithmetic and copies ran while one was open for 2% of the time, Pallas kernels for 10%

commit v1 on v0

--- a/solution.py
+++ b/solution.py
@@ -105,10 +105,10 @@
     held = held.astype(BF)
     for j in range(2 * rank // extra):
         piece = held[j * extra : (j + 1) * extra, :]
-        out[cap : cap + extra, j * n : (j + 1) * n] = piece
-    far_copy = start(out.at[pl.ds(cap, extra), :], far_o, sems.at[3])
+        out[:extra, j * n : (j + 1) * n] = piece
+    far_copy = start(out.at[pl.ds(0, extra), :], far_o, sems.at[3])
     copies[1].wait()
-    out[:cap, :] = dot(pick, tokens_v[...]).astype(BF)
+    out[extra : extra + cap, :] = dot(pick, tokens_v[...]).astype(BF)
     copies[2].wait()
     out[cap + extra :, :] = (dot(pick, cotangent_v[...]) * gate).astype(BF)
     start(out, out_o, sems.at[4]).wait()
@@ -137,7 +137,7 @@
 
 
 N_Y = 4
-CHUNK = 1024
+CHUNK = 2048
 
 
 def block_of(place, k, other):
@@ -200,9 +200,9 @@
     def fetch(source, target):
         return start(source, target, in_sems.at[next(count)])
 
-    sources = [b.at[pl.ds(cap, extra), :] for b in blocks] + list(fars)
+    sources = [b.at[pl.ds(0, extra), :] for b in blocks] + list(fars)
     got_first = [fetch(a, packed.at[pl.ds(i * extra, extra), :]) for i, a in enumerate(sources)]
-    got_x = [fetch(b.at[pl.ds(0, cap), :], xs.at[pl.ds(i * cap, cap), :]) for i, b in enumerate(blocks)]
+    got_x = [fetch(b.at[pl.ds(extra, cap), :], xs.at[pl.ds(i * cap, cap), :]) for i, b in enumerate(blocks)]
     got_gate_up = fetch(gate_up, weights.at[pl.ds(0, 2 * h), :])
     got_down = fetch(down, down_v)
 
@@ -269,9 +269,9 @@
 
 
 def rest_kernel(cap, place, *refs):
-    near, far_x, far_d, refs = refs[:6], refs[6:8], refs[8:10], refs[10:]
+    near, far, refs = refs[:6], refs[6:8], refs[8:]
     (gate_n, up_n, low_n, gate_up, down, first, second), refs = refs[:7], refs[7:]
-    (low_a, low_b, part, second_o, mine, other), refs = refs[:6], refs[6:]
+    (low_t, part, second_o, mine, other), refs = refs[:5], refs[5:]
     xs, ds, gate_v, up_v, low_v, weights, down_v, hidden, grads, outs, in_sems, out_sems = refs
     h, rank, width = down.shape[0], second.shape[1], down.shape[1]
     n = 2 * N_Y
@@ -289,14 +289,15 @@
         for j, k in enumerate((0, 1, 3)):
             place_of[o * N_Y + k] = (False, 3 * o + j)
         place_of[o * N_Y + 2] = (True, o)
-    last = near[0].shape[0] - cap
-    got_x = [fetch(far_x[o].at[pl.ds(0, cap), :], xs.at[rows_of(o), :]) for o in range(2)]
+    extra = near[0].shape[0] - 2 * cap
+    got_x = [fetch(far[o].at[pl.ds(0, cap), :], xs.at[rows_of(o), :]) for o in range(2)]
     got_weights = [fetch(gate_up, weights.at[pl.ds(0, 2 * h), :]), fetch(first, weights.at[pl.ds(2 * h, 2 * rank), :])]
     got_down = fetch(down, down_v)
     got_d, got_pre, saved = [], [], []
     for i in range(n):
         is_far, j = place_of[i]
-        got_d.append(fetch(far_d[j] if is_far else near[j].at[pl.ds(last, cap), :], ds.at[rows_of(i), :]))
+        source = far[j].at[pl.ds(cap, cap), :] if is_far else near[j].at[pl.ds(extra + cap, cap), :]
+        got_d.append(fetch(source, ds.at[rows_of(i), :]))
     for i in range(n):
         is_far, j = place_of[i]
         if not is_far:
@@ -307,7 +308,7 @@
     for i in range(n):
         is_far, j = place_of[i]
         at = pl.multiple_of(block_of(place, i % N_Y, i >= N_Y) * cap, cap)
-        source = (far_x if is_far else near)[j].at[pl.ds(0, cap), cols]
+        source = far[j].at[pl.ds(0, cap), cols] if is_far else near[j].at[pl.ds(extra, cap), cols]
         saved.append(start(source, part.at[pl.ds(at, cap), :], out_sems.at[8 + i]))
 
     wait(got_x)
@@ -355,30 +356,27 @@
         ours = grad_low[k * cap : (k + 1) * cap, :].astype(F32)
         theirs = grad_low[(N_Y + k) * cap : (N_Y + k + 1) * cap, :].astype(F32)
         rows = jnp.concatenate([jnp.where(straight, ours, theirs), jnp.where(straight, theirs, ours)], axis=0)
-        turned = dot(order, rows.astype(BF), NT).astype(BF)
         at = pl.multiple_of(lax.div(block_of(place, k, False), 2) * 2 * cap, 2 * cap)
-        low_a[:, pl.ds(at, 2 * cap)] = turned[: lanes // 2, :]
-        low_b[:, pl.ds(at, 2 * cap)] = turned[lanes // 2 :, :]
+        low_t[:, pl.ds(at, 2 * cap)] = dot(order, rows.astype(BF), NT).astype(BF)
     finish_chunks(outs, mine, other, out_sems)
     wait(saved)
 
 
-def rest(cap, place, near, far_x, far_d, pre_near, gate_up, down, first, second):
+def rest(cap, place, near, far, pre_near, gate_up, down, first, second):
     width, h, both = down.shape[1], down.shape[0], 2 * second.shape[1]
     rows = 2 * N_Y * cap
     return call(
         functools.partial(rest_kernel, cap),
         [
-            shape((both // 2, rows)),
-            shape((both // 2, rows)),
+            shape((both, rows)),
             shape((rows, width // (2 * N_Y))),
             shape(second.shape, F32),
             shape((rows // 2 + cap, width)),
             shape((rows // 2 + cap, width)),
         ],
-        [place, *near, *far_x, *far_d, *pre_near, gate_up, down, first, second],
-        [SMEM] + [HBM] * 16 + [VMEM],
-        [VMEM, VMEM, HBM, VMEM, HBM, HBM],
+        [place, *near, *far, *pre_near, gate_up, down, first, second],
+        [SMEM] + [HBM] * 14 + [VMEM],
+        [VMEM, HBM, VMEM, HBM, HBM],
         scratch=[
             pltpu.VMEM((2 * cap, width), BF),
             pltpu.VMEM((rows, width), BF),
@@ -399,7 +397,7 @@
 
 
 def pack_kernel(cap, n_z, place, *refs):
-    sources, outs, (own, came, packed, sems, out_sems) = refs[:4], refs[4 : 4 + 2 * N_Y], refs[4 + 2 * N_Y :]
+    sources, outs, (own, came, packed, sems, out_sems) = refs[:4], refs[4 : 4 + N_Y], refs[4 + N_Y :]
     n = N_Y
     core, x = place[1], place[2]
     lanes = own.shape[2] // (n_z * n)
@@ -427,10 +425,11 @@
         for to in range(n):
             for slot in range(n):
                 i, q = (to, slot) if straight else (slot, to)
+                at = (2 * slot + which) * cap
                 for z in range(n_z):
-                    rows, cols = slice(slot * cap, (slot + 1) * cap), slice(z * lanes, (z + 1) * lanes)
-                    packed[which * n + to, rows, cols] = block(which, i, q, z)
-            start(packed.at[which * n + to], outs[which * n + to], out_sems.at[which * n + to])
+                    packed[to, at : at + cap, z * lanes : (z + 1) * lanes] = block(which, i, q, z)
+            if which:
+                start(packed.at[to], outs[to], out_sems.at[to])
 
     for which in range(2):
         wait(copies[which * 2 * n : (which + 1) * 2 * n])
@@ -443,29 +442,28 @@
         def _():
             store(which, False)
 
-    for to in range(2 * n):
+    for to in range(n):
         pltpu.make_async_copy(packed.at[to], outs[to], out_sems.at[to]).wait()
 
 
 def add_and_pack(cap, sources, place):
     n, n_z = N_Y, lax.axis_size("z")
     width = sources[0].shape[1]
-    parts = call(
+    return call(
         functools.partial(pack_kernel, cap, n_z),
-        [shape((n * cap, width // n))] * (2 * n),
+        [shape((2 * n * cap, width // n))] * n,
         [place, *sources],
         [SMEM] + [HBM] * len(sources),
-        [HBM] * (2 * n),
+        [HBM] * n,
         scratch=[pltpu.VMEM((2, n * cap, width), BF)] * 2
         + [
-            pltpu.VMEM((2 * n, n * cap, width // n), BF),
+            pltpu.VMEM((n, 2 * n * cap, width // n), BF),
             pltpu.SemaphoreType.DMA((4 * n,)),
-            pltpu.SemaphoreType.DMA((2 * n,)),
+            pltpu.SemaphoreType.DMA((n,)),
         ],
         limit=20,
         name="add_and_pack",
     )
-    return parts[:n], parts[n:]
 
 
 def total(parts):
@@ -530,12 +528,11 @@
     front = ahead(own, -1)
     own_s = swap(own)
     far_first = ahead(far_first, 2)
+    far_first_s = swap(far_first)
+    behind, front, _ = lax.optimization_barrier((behind, front, far_first_s))
     front_s = swap(behind)
     behind_s = swap(front)
-    far_first_s = swap(far_first)
-    relayed = tie(behind, front_s, behind_s, far_first_s)
-    far_x = ahead(relayed[: own.shape[0] - cap])
-    far_d = ahead(relayed[own.shape[0] - cap :])
+    far = ahead(tie(behind[own.shape[0] - 2 * cap :], front_s, behind_s))
 
     weights = (gate_up, down_weight)
     near = [own, front, behind, own_s, front_s, behind_s]
@@ -543,32 +540,29 @@
         cap, (0, 1, 3), place, near, [far_first, far_first_s], *weights, adapter_second_factors
     )
     came_near = swap(other_near)
-    far_x, far_d, _ = lax.optimization_barrier((far_x, far_d, mine_near))
-    far_x_s = swap(far_x)
-    far_d_s = swap(far_d)
-    low_a, low_b, x_part, second_gradient, mine_rest, other_rest = rest(
-        cap, place, near, [far_x, far_x_s], [far_d, far_d_s], pre_near, *weights, first, adapter_second_factors
-    )
-    came_rest = swap(other_rest)
+    far = tie(far, mine_near)
+    far_s = swap(far)
+    low_t, x_part, second_gradient, mine_rest, other_rest = rest(
+        cap, place, near, [far, far_s], pre_near, *weights, first, adapter_second_factors
+    )
 
     def crossing(axis, bit):
         return [(i, i ^ bit) for i in range(lax.axis_size(axis))]
 
-    cols = low_a.shape[0] // 2
-    pair = low_a.astype(F32) + lax.ppermute(low_b, "x", crossing("x", 2)).astype(F32)
-    low_sum = pair[:cols] + lax.ppermute(pair[cols:].astype(BF), "x", crossing("x", 1)).astype(F32)
-    out_parts, in_parts = add_and_pack(cap, [mine_near, mine_rest, came_near, came_rest], place)
-    out_got = first_moves(out_parts)
-    in_got = first_moves(in_parts)
-    out_once = total(out_got).astype(BF)
-    mixed_rows = total(second_moves(out_once, n_y)) * row_gate
-    low_sum = low_sum + swap(tie(low_sum, *in_got))
-    in_once = tie(total(in_got).astype(BF), low_sum)
-    in_moved = second_moves(in_once, n_y)
-    low_sum = tie(low_sum, in_moved[1])
+    cols = low_t.shape[0] // n_x
+    low_sum = low_t.astype(F32) + swap(low_t).astype(F32)
+    came_rest = swap(other_rest)
+    sent = low_sum[2 * cols :].astype(BF)
+    moved = lax.ppermute(sent, "x", crossing("x", 2))
+    parts = add_and_pack(cap, [mine_near, mine_rest, came_near, came_rest], place)
+    got = first_moves(parts)
+    got_again = second_moves(total(got).astype(BF), n_y)
+    pair = tie(low_sum[: 2 * cols], *got) + moved.astype(F32)
+    low_sum = lax.ppermute(pair[cols:].astype(BF), "x", crossing("x", 1)).astype(F32)
+    low_sum = tie(pair[:cols], got_again[1]) + low_sum
     low_sum = low_sum + lax.ppermute(low_sum, "y", crossing("y", 2))
-    in_rows = tie(total(in_moved), low_sum)
-    mixed, token_gradient = to_tokens([mixed_rows, in_rows], combine)
+    sums = total(got_again)
+    mixed, token_gradient = to_tokens([sums[:cap] * row_gate, sums[cap:]], combine)
     summed = (low_sum + lax.ppermute(low_sum, "y", crossing("y", 1))).astype(BF)
     first_gradient = dot(summed, x_part).reshape(2, member_cols, part_width).transpose(0, 2, 1)
     return (mixed, token_gradient, first_gradient, second_gradient)

time: 171 us -> 163 us (0.953); the launches traced: 171 us -> 161 us
  starting transfers between devices: 49.2 us -> 34.5 us
  waiting for transfers between devices: 69.5 us -> 75.3 us
    ppermute x12 -> x6, starting transfers between devices: 22.4 us -> 8.36 us  [crossed(): return lax.ppermute(values, ('y', 'core', 'x'), pairs)]
    ppermute x12 -> x6, waiting for transfers between devices: 9.51 us -> 23.1 us  [crossed(): return lax.ppermute(values, ('y', 'core', 'x'), pairs)]
    ppermute x9 -> x8, waiting for transfers between devices: 9.87 us -> 17.6 us  [swap(): return lax.ppermute(values, 'core', [(0, 1), (1, 0)])]
    ppermute x5 -> x4, waiting for transfers between devices: 34.2 us -> 27.3 us  [ahead(): return lax.ppermute(values, ('y', 'core'), pairs)]
    all_to_all x1, waiting for transfers between devices: 9.49 us -> 5.23 us  [to_tokens(): came = lax.all_to_all(jnp.concatenate(sent, axis=2), 'z', 0, 0, tiled=True)]
    ppermute x1, waiting for transfers between devices: 4.17 us -> 0.01 us  [shards(): lax.ppermute(pair[cols:].astype(BF), 'x', crossing('x', 1)).astype(F32)]
    ppermute x9 -> x8, starting transfers between devices: 6.12 us -> 2.08 us  [swap(): return lax.ppermute(values, 'core', [(0, 1), (1, 0)])]
    all_to_all x1, starting transfers between devices: 6 us -> 8.47 us  [to_tokens(): came = lax.all_to_all(jnp.concatenate(sent, axis=2), 'z', 0, 0, tiled=True)]
  transfers between devices with their start and end apart: 31 -> 23, of which waited for: 13 -> 18; matrix products, arithmetic and copies ran while one was open for 2% -> 2% of each run, Pallas kernels for 10% -> 8%
where the time goes in v1:
time: 163 us; the launch traced here: 161 us
  waiting for transfers between devices  75.3 us (46%)
  Pallas kernels  40.8 us (25%)
  starting transfers between devices  34.5 us (21%)
  local copies, waits for them, and re-layouts  5.44 us (3%)
  other arithmetic  2.76 us (2%)
    pallas_call x4, Pallas kernels, call(): pl.pallas_call(kernel, out_shape=out_shape, in_specs=in_specs, out_specs=...  40.8 us
    ppermute x4, waiting for transfers between devices, ahead(): return lax.ppermute(values, ('y', 'core'), pairs)  27.3 us
    ppermute x6, waiting for transfers between devices, crossed(): return lax.ppermute(values, ('y', 'core', 'x'), pairs)  23.1 us
    ppermute x8, waiting for transfers between devices, swap(): return lax.ppermute(values, 'core', [(0, 1), (1, 0)])  17.6 us
    all_to_all x1, starting transfers between devices, to_tokens(): came = lax.all_to_all(jnp.concatenate(sent, axis=2), 'z', 0, 0, tiled=True)  8.47 us
    ppermute x6, starting transfers between devices, crossed(): return lax.ppermute(values, ('y', 'core', 'x'), pairs)  8.36 us
    ppermute x4, starting transfers between devices, ahead(): return lax.ppermute(values, ('y', 'core'), pairs)  5.6 us
    all_to_all x1, waiting for transfers between devices, to_tokens(): came = lax.all_to_all(jnp.concatenate(sent, axis=2), 'z', 0, 0, tiled=True)  5.23 us
  transfers between devices with their start and end apart: 23, of which 18 were waited for; matrix products, arithmetic and copies ran while one was open for 2% of the time, Pallas kernels for 8%

profile of v1, /device:TPU:8, one launch (start us, length us, event | category | flops | bytes accessed | tf_op | source)
XLA Modules:
  0.0 160.8 jit_solution(7985223994245113683)
XLA Ops:
  1.3 4.7 %expert_rows.1 = (bf16[144,4096]{1,0:T(8,128)(2,1)}, bf16[16,4096]{1,0:T(8,128)(2,1)}, f32[64,1]{1,0:T(8,128)}) custom-call(s32[4]{0:T(128)} %pad_add_fusion.place, bf16[128,4096]{1,0:T(8,128)(2,1)} %tokens.1, bf16[128,4096]{1,0:T(8,128)(2,1)} %cotangent.1, bf16[2,512,512]{2,1,0:T(8,128)(2,1)} %first.1, s32[2,128]{1,0:T(2,128)} %bitcast.34, f32[2,128]{1,0:T(2,128)} %bitcast.35), custom_call_target="tpu_custom_call" | custom-call | tf_op jit(solution)/shard_map/expert_rows/pallas_call | solution.py:32
  6.0 2.2 %collective-permute-start.1 = (bf16[144,4096]{1,0:T(8,128)(2,1)}, bf16[144,4096]{1,0:T(8,128)(2,1)S(1)}, u32[]{:S(2)}, u32[]{:S(2)}) collective-permute-start(bf16[144,4096]{1,0:T(8,128)(2,1)} %get-tuple-element.28.refs_0_), channel_id=1, source_target_pairs={{0,192},{32,96},{64,0},{96,160},{128,64},{160,224},{192,128},{224,... | collective-permute-start | bytes 3538952 | tf_op jit(solution)/shard_map/ppermute | solution.py:61
  8.3 3.3 %collective-permute-start.2 = (bf16[16,4096]{1,0:T(8,128)(2,1)}, bf16[16,4096]{1,0:T(8,128)(2,1)S(1)}, u32[]{:S(2)}, u32[]{:S(2)}) collective-permute-start(bf16[16,4096]{1,0:T(8,128)(2,1)} %get-tuple-element.29), channel_id=1, source_target_pairs={{0,128},{32,160},{64,192},{96,224},{128,0},{160,32},{192,64},{224,... | collective-permute-start | bytes 393224 | tf_op jit(solution)/shard_map/ppermute | solution.py:61
  11.6 27.2 %collective-permute-done.2.refs_6_ = bf16[16,4096]{1,0:T(8,128)(2,1)S(1)} collective-permute-done((bf16[16,4096]{1,0:T(8,128)(2,1)}, bf16[16,4096]{1,0:T(8,128)(2,1)S(1)}, u32[]{:S(2)}, u32[]{:S(2)}) %collective-permute-start.2) | collective-permute-done | bytes 131104 | tf_op jit(solution)/shard_map/ppermute | solution.py:61
  38.8 1.3 collective-permute-done.3.refs_7_
  41.0 2.1 %collective-permute-done.6.refs_5_ = bf16[144,4096]{1,0:T(8,128)(2,1)S(1)} collective-permute-done((bf16[144,4096]{1,0:T(8,128)(2,1)S(1)}, bf16[144,4096]{1,0:T(8,128)(2,1)S(1)}, u32[]{:S(2)}, u32[]{:S(2)}) %collective-permute-start.6) | collective-permute-done | bytes 1179680 | tf_op jit(solution)/shard_map/ppermute | solution.py:55
  43.1 3.4 %collective-permute-done.5.refs_4_ = bf16[144,4096]{1,0:T(8,128)(2,1)S(1)} collective-permute-done((bf16[144,4096]{1,0:T(8,128)(2,1)S(1)}, bf16[144,4096]{1,0:T(8,128)(2,1)S(1)}, u32[]{:S(2)}, u32[]{:S(2)}) %collective-permute-start.5) | collective-permute-done | bytes 1179680 | tf_op jit(solution)/shard_map/ppermute | solution.py:55
  47.5 1.1 copy-done.12
  48.6 12.7 %forward_rows.1 = (f32[384,336]{1,0:T(8,128)}, f32[384,336]{1,0:T(8,128)}, bf16[384,128]{1,0:T(8,128)(2,1)}, bf16[192,4096]{1,0:T(8,128)(2,1)}, bf16[192,4096]{1,0:T(8,128)(2,1)}, /*index=5*/bf16[128,4096]{1,0:T(8,128)(2,1)}) custom-call(s32[4]{0:T(128)} %pad_add_fusion.place, bf16[144,4096]{1,0:T(8,128)(2,1)} %get-tuple-element.28.refs_0_, ...), custom_call_target="tpu_custom_call" | custom-call | flops 10000000000 | tf_op jit(solution)/shard_map/forward_rows/pallas_call | solution.py:32
  61.8 2.7 %collective-permute-done.8.refs_7_ = bf16[128,4096]{1,0:T(8,128)(2,1)S(1)} collective-permute-done((bf16[128,4096]{1,0:T(8,128)(2,1)}, bf16[128,4096]{1,0:T(8,128)(2,1)S(1)}, u32[]{:S(2)}, u32[]{:S(2)}) %collective-permute-start.8) | collective-permute-done | bytes 1048608 | tf_op jit(solution)/shard_map/ppermute | solution.py:55
  64.5 1.0 copy-done.13
  65.5 19.3 %rest_rows.1 = (bf16[128,512]{1,0:T(8,128)(2,1)}, bf16[512,512]{1,0:T(8,128)(2,1)}, f32[2,64,336]{2,1,0:T(8,128)}, bf16[320,4096]{1,0:T(8,128)(2,1)}, bf16[320,4096]{1,0:T(8,128)(2,1)}) custom-call(s32[4]{0:T(128)} %pad_add_fusion.place, bf16[144,4096]{1,0:T(8,128)(2,1)} %get-tuple-element.28.refs_0_, bf16[144,4096]{1,0:T(8,128)(2,1)} %copy-done.9, ...), custom_call_target="tpu_custom_call" | custom-call | flops 10000000000 | tf_op jit(solution)/shard_map/rest_rows/pallas_call | solution.py:32
  85.4 6.6 %collective-permute-done.9.refs_2_ = bf16[192,4096]{1,0:T(8,128)(2,1)S(1)} collective-permute-done((bf16[192,4096]{1,0:T(8,128)(2,1)S(1)}, bf16[192,4096]{1,0:T(8,128)(2,1)S(1)}, u32[]{:S(2)}, u32[]{:S(2)}) %collective-permute-start.9) | collective-permute-done | bytes 1572896 | tf_op jit(solution)/shard_map/ppermute | solution.py:55
  92.2 1.7 %copy-done = bf16[320,4096]{1,0:T(8,128)(2,1)S(1)} copy-done((bf16[320,4096]{1,0:T(8,128)(2,1)S(1)}, bf16[320,4096]{1,0:T(8,128)(2,1)}, u32[]{:S(2)}) %copy-start) | copy-done | bytes 2621464
  93.9 4.1 %add_and_pack.1 = (bf16[512,1024]{1,0:T(8,128)(2,1)S(1)}, bf16[512,1024]{1,0:T(8,128)(2,1)S(1)}, bf16[512,1024]{1,0:T(8,128)(2,1)S(1)}, bf16[512,1024]{1,0:T(8,128)(2,1)S(1)}) custom-call(s32[4]{0:T(128)S(1)} %copy-done.2, bf16[192,4096]{1,0:T(8,128)(2,1)S(1)} %copy-done.1, bf16[320,4096]{1,0:T(8,128)(2,1)S(1)} %copy-done, ...), custom_call_target="tpu_custom_call" | custom-call | tf_op jit(solution)/shard_map/add_and_pack/pallas_call | solution.py:32
  98.0 1.0 collective-permute-start.11
  99.0 3.0 %collective-permute-start.12 = (bf16[512,1024]{1,0:T(8,128)(2,1)S(1)}, bf16[512,1024]{1,0:T(8,128)(2,1)S(1)}, u32[]{:S(2)}, u32[]{:S(2)}) collective-permute-start(bf16[512,1024]{1,0:T(8,128)(2,1)S(1)} %get-tuple-element.44), channel_id=1, source_target_pairs={{0,128},{1,129},{2,130},{3,131},{32,34},{33,35},{34,32},{35,33},{6... | collective-permute-start | bytes 3145736 | tf_op jit(solution)/shard_map/ppermute | solution.py:72
  103.1 1.0 collective-permute-done.17
  104.1 3.1 %collective-permute-start.18 = (bf16[64,512]{1,0:T(8,128)(2,1)S(1)}, bf16[64,512]{1,0:T(8,128)(2,1)S(1)}, u32[]{:S(2)}, u32[]{:S(2)}) collective-permute-start(bf16[64,512]{1,0:T(8,128)(2,1)S(1)} %slice.78), channel_id=1, source_target_pairs={{0,2},{1,3},{2,0},{3,1},{4,6},{5,7},{6,4},{7,5},{8,10},{9,11},{10,... | collective-permute-start | bytes 196616 | tf_op jit(solution)/shard_map/ppermute | solution.py:556
  107.2 5.7 %collective-permute-done.11 = bf16[512,1024]{1,0:T(8,128)(2,1)S(1)} collective-permute-done((bf16[512,1024]{1,0:T(8,128)(2,1)S(1)}, bf16[512,1024]{1,0:T(8,128)(2,1)S(1)}, u32[]{:S(2)}, u32[]{:S(2)}) %collective-permute-start.11) | collective-permute-done | bytes 1048608 | tf_op jit(solution)/shard_map/ppermute | solution.py:72
  112.9 2.5 %collective-permute-done.12 = bf16[512,1024]{1,0:T(8,128)(2,1)S(1)} collective-permute-done((bf16[512,1024]{1,0:T(8,128)(2,1)S(1)}, bf16[512,1024]{1,0:T(8,128)(2,1)S(1)}, u32[]{:S(2)}, u32[]{:S(2)}) %collective-permute-start.12) | collective-permute-done | bytes 1048608 | tf_op jit(solution)/shard_map/ppermute | solution.py:72
  115.4 11.1 %collective-permute-done.13 = bf16[512,1024]{1,0:T(8,128)(2,1)S(1)} collective-permute-done((bf16[512,1024]{1,0:T(8,128)(2,1)S(1)}, bf16[512,1024]{1,0:T(8,128)(2,1)S(1)}, u32[]{:S(2)}, u32[]{:S(2)}) %collective-permute-start.13) | collective-permute-done | bytes 1048608 | tf_op jit(solution)/shard_map/ppermute | solution.py:72
  127.6 1.1 collective-permute-start.14
  128.7 1.6 collective-permute-start.19
  130.3 1.8 %collective-permute-start.16 = (bf16[128,1024]{1,0:T(8,128)(2,1)S(1)}, bf16[128,1024]{1,0:T(8,128)(2,1)S(1)}, u32[]{:S(2)}, u32[]{:S(2)}) collective-permute-start(bf16[128,1024]{1,0:T(8,128)(2,1)S(1)} %get-tuple-element.53), channel_id=1, source_target_pairs={{0,3},{1,0},{2,1},{3,2},{32,96},{33,97},{34,98},{35,99},{64,67},{6... | collective-permute-start | bytes 786440 | tf_op jit(solution)/shard_map/ppermute | solution.py:72
  133.0 2.2 %collective-permute-done.14 = bf16[128,1024]{1,0:T(8,128)(2,1)S(1)} collective-permute-done((bf16[128,1024]{1,0:T(8,128)(2,1)S(1)}, bf16[128,1024]{1,0:T(8,128)(2,1)S(1)}, u32[]{:S(2)}, u32[]{:S(2)}) %collective-permute-start.14) | collective-permute-done | bytes 262176 | tf_op jit(solution)/shard_map/ppermute | solution.py:72
  135.2 3.1 %collective-permute-start.20 = (f32[32,512]{1,0:T(8,128)S(1)}, f32[32,512]{1,0:T(8,128)S(1)}, u32[]{:S(2)}, u32[]{:S(2)}) collective-permute-start(f32[32,512]{1,0:T(8,128)S(1)} %convert_add_fusion.3), channel_id=1, source_target_pairs={{0,128},{64,192},{128,0},{192,64},{1,129},{65,193},{129,1},{193,65... | collective-permute-start | bytes 196616 | tf_op jit(solution)/shard_map/ppermute | solution.py:563
  138.8 1.1 collective-permute-done.15
  140.9 8.5 %all-to-all-start = ((bf16[8,64,256]{2,1,0:T(8,128)(2,1)}), bf16[8,64,256]{2,1,0:T(8,128)(2,1)S(1)}, u32[]{:S(2)}, u32[]{:S(2)}) async-start(bf16[8,64,256]{2,1,0:T(8,128)(2,1)} %pad_maximum_fusion), calls=%async_computation | async-start | bytes 524288 | tf_op jit(solution)/shard_map/all_to_all | solution.py:491
  149.4 2.2 %collective-permute-start.21 = (f32[32,512]{1,0:T(8,128)S(1)}, f32[32,512]{1,0:T(8,128)S(1)}, u32[]{:S(2)}, u32[]{:S(2)}) collective-permute-start(f32[32,512]{1,0:T(8,128)S(1)} %add.42), channel_id=1, source_target_pairs={{0,64},{64,0},{128,192},{192,128},{1,65},{65,1},{129,193},{193,129... | collective-permute-start | bytes 196616 | tf_op jit(solution)/shard_map/ppermute | solution.py:566
  151.7 2.1 %collective-permute-done.21 = f32[32,512]{1,0:T(8,128)S(1)} collective-permute-done((f32[32,512]{1,0:T(8,128)S(1)}, f32[32,512]{1,0:T(8,128)S(1)}, u32[]{:S(2)}, u32[]{:S(2)}) %collective-permute-start.21) | collective-permute-done | bytes 65568 | tf_op jit(solution)/shard_map/ppermute | solution.py:566
  154.7 5.2 %all-to-all-done = bf16[8,64,256]{2,1,0:T(8,128)(2,1)S(1)} async-done(((bf16[8,64,256]{2,1,0:T(8,128)(2,1)}), bf16[8,64,256]{2,1,0:T(8,128)(2,1)S(1)}, u32[]{:S(2)}, u32[]{:S(2)}) %all-to-all-start) | async-done | bytes 262176 | tf_op jit(solution)/shard_map/all_to_all | solution.py:491
  (71 shorter events, 10.1 us)
Async XLA Ops:
  6.0 34.2 %collective-permute-start.1 = (bf16[144,4096]{1,0:T(8,128)(2,1)}, bf16[144,4096]{1,0:T(8,128)(2,1)S(1)}, u32[]{:S(2)}, u32[]{:S(2)}) collective-permute-start(bf16[144,4096]{1,0:T(8,128)(2,1)} %get-tuple-element.28.refs_0_), channel_id=1, source_target_pairs={{0,192},{32,96},{64,0},{96,160},{128,64},{160,224},{192,128},{224,... | collective-permute-start | bytes 3538952 | tf_op jit(solution)/shard_map/ppermute | solution.py:61
  8.3 31.9 %collective-permute-start = (bf16[144,4096]{1,0:T(8,128)(2,1)}, bf16[144,4096]{1,0:T(8,128)(2,1)S(1)}, u32[]{:S(2)}, u32[]{:S(2)}) collective-permute-start(bf16[144,4096]{1,0:T(8,128)(2,1)} %get-tuple-element.28.refs_0_), channel_id=1, source_target_pairs={{0,64},{32,224},{64,128},{96,32},{128,192},{160,96},{192,0},{224,1... | collective-permute-start | bytes 3538952 | tf_op jit(solution)/shard_map/ppermute | solution.py:61
  8.3 30.6 %collective-permute-start.2 = (bf16[16,4096]{1,0:T(8,128)(2,1)}, bf16[16,4096]{1,0:T(8,128)(2,1)S(1)}, u32[]{:S(2)}, u32[]{:S(2)}) collective-permute-start(bf16[16,4096]{1,0:T(8,128)(2,1)} %get-tuple-element.29), channel_id=1, source_target_pairs={{0,128},{32,160},{64,192},{96,224},{128,0},{160,32},{192,64},{224,... | collective-permute-start | bytes 393224 | tf_op jit(solution)/shard_map/ppermute | solution.py:61
  38.8 9.8 %copy-start.14 = (bf16[16,4096]{1,0:T(8,128)(2,1)}, bf16[16,4096]{1,0:T(8,128)(2,1)S(1)}, u32[]{:S(2)}) copy-start(bf16[16,4096]{1,0:T(8,128)(2,1)S(1)} %collective-permute-done.2.refs_6_) | copy-start | bytes 393220
  38.8 1.3 collective-permute-start.3
  40.2 8.4 %copy-start.15 = (bf16[16,4096]{1,0:T(8,128)(2,1)}, bf16[16,4096]{1,0:T(8,128)(2,1)S(1)}, u32[]{:S(2)}) copy-start(bf16[16,4096]{1,0:T(8,128)(2,1)S(1)} %collective-permute-done.3.refs_7_) | copy-start | bytes 393220
  40.2 8.4 %copy-start.9 = (bf16[144,4096]{1,0:T(8,128)(2,1)}, bf16[144,4096]{1,0:T(8,128)(2,1)S(1)}, u32[]{:S(2)}) copy-start(bf16[144,4096]{1,0:T(8,128)(2,1)S(1)} %collective-permute-done.1.refs_1_) | copy-start | bytes 3538948
  40.2 8.4 %copy-start.3 = (bf16[144,4096]{1,0:T(8,128)(2,1)}, bf16[144,4096]{1,0:T(8,128)(2,1)S(1)}, u32[]{:S(2)}) copy-start(bf16[144,4096]{1,0:T(8,128)(2,1)S(1)} %collective-permute-done.refs_2_) | copy-start | bytes 3538948
  40.2 2.9 %collective-permute-start.6 = (bf16[144,4096]{1,0:T(8,128)(2,1)S(1)}, bf16[144,4096]{1,0:T(8,128)(2,1)S(1)}, u32[]{:S(2)}, u32[]{:S(2)}) collective-permute-start(bf16[144,4096]{1,0:T(8,128)(2,1)S(1)} %collective-permute-done.1.refs_1_), channel_id=1, source_target_pairs={{0,32},{32,0},{1,33},{33,1},{2,34},{34,2},{3,35},{35,3},{4,36},{36... | collective-permute-start | bytes 3538952 | tf_op jit(solution)/shard_map/ppermute | solution.py:55
  40.4 6.1 %collective-permute-start.5 = (bf16[144,4096]{1,0:T(8,128)(2,1)S(1)}, bf16[144,4096]{1,0:T(8,128)(2,1)S(1)}, u32[]{:S(2)}, u32[]{:S(2)}) collective-permute-start(bf16[144,4096]{1,0:T(8,128)(2,1)S(1)} %collective-permute-done.refs_2_), channel_id=1, source_target_pairs={{0,32},{32,0},{1,33},{33,1},{2,34},{34,2},{3,35},{35,3},{4,36},{36... | collective-permute-start | bytes 3538952 | tf_op jit(solution)/shard_map/ppermute | solution.py:55
  40.8 5.9 %collective-permute-start.4 = (bf16[144,4096]{1,0:T(8,128)(2,1)}, bf16[144,4096]{1,0:T(8,128)(2,1)S(1)}, u32[]{:S(2)}, u32[]{:S(2)}) collective-permute-start(bf16[144,4096]{1,0:T(8,128)(2,1)} %get-tuple-element.28.refs_0_), channel_id=1, source_target_pairs={{0,32},{32,0},{1,33},{33,1},{2,34},{34,2},{3,35},{35,3},{4,36},{36... | collective-permute-start | bytes 3538952 | tf_op jit(solution)/shard_map/ppermute | solution.py:55
  46.5 14.9 %collective-permute-start.7 = (bf16[128,4096]{1,0:T(8,128)(2,1)S(1)}, bf16[128,4096]{1,0:T(8,128)(2,1)}, u32[]{:S(2)}, u32[]{:S(2)}) collective-permute-start(bf16[128,4096]{1,0:T(8,128)(2,1)S(1)} %slice.42), channel_id=1, source_target_pairs={{0,64},{32,224},{64,128},{96,32},{128,192},{160,96},{192,0},{224,1... | collective-permute-start | bytes 3145736 | tf_op jit(solution)/shard_map/ppermute | solution.py:61
  61.4 3.1 %collective-permute-start.8 = (bf16[128,4096]{1,0:T(8,128)(2,1)}, bf16[128,4096]{1,0:T(8,128)(2,1)S(1)}, u32[]{:S(2)}, u32[]{:S(2)}) collective-permute-start(bf16[128,4096]{1,0:T(8,128)(2,1)} %collective-permute-done.7.refs_6_), channel_id=1, source_target_pairs={{0,32},{32,0},{1,33},{33,1},{2,34},{34,2},{3,35},{35,3},{4,36},{36... | collective-permute-start | bytes 3145736 | tf_op jit(solution)/shard_map/ppermute | solution.py:55
  65.5 19.5 %copy-start.8 = (bf16[192,4096]{1,0:T(8,128)(2,1)S(1)}, bf16[192,4096]{1,0:T(8,128)(2,1)}, u32[]{:S(2)}) copy-start(bf16[192,4096]{1,0:T(8,128)(2,1)} %get-tuple-element.40) | copy-start | bytes 4718596
  65.5 26.7 %copy-start.1 = (bf16[192,4096]{1,0:T(8,128)(2,1)S(1)}, bf16[192,4096]{1,0:T(8,128)(2,1)}, u32[]{:S(2)}) copy-start(bf16[192,4096]{1,0:T(8,128)(2,1)} %get-tuple-element.32.refs_0_) | copy-start | bytes 4718596
  65.5 26.7 %copy-start.2 = (s32[4]{0:T(128)S(1)}, s32[4]{0:T(128)}, u32[]{:S(2)}) copy-start(s32[4]{0:T(128)} %pad_add_fusion.place) | copy-start | bytes 52
  84.8 7.4 %collective-permute-start.10 = (bf16[320,4096]{1,0:T(8,128)(2,1)}, bf16[320,4096]{1,0:T(8,128)(2,1)S(1)}, u32[]{:S(2)}, u32[]{:S(2)}) collective-permute-start(bf16[320,4096]{1,0:T(8,128)(2,1)} %get-tuple-element.41), channel_id=1, source_target_pairs={{0,32},{32,0},{1,33},{33,1},{2,34},{34,2},{3,35},{35,3},{4,36},{36... | collective-permute-start | bytes 7864328 | tf_op jit(solution)/shard_map/ppermute | solution.py:55
  85.0 7.0 %collective-permute-start.9 = (bf16[192,4096]{1,0:T(8,128)(2,1)S(1)}, bf16[192,4096]{1,0:T(8,128)(2,1)S(1)}, u32[]{:S(2)}, u32[]{:S(2)}) collective-permute-start(bf16[192,4096]{1,0:T(8,128)(2,1)S(1)} %copy-done.8), channel_id=1, source_target_pairs={{0,32},{32,0},{1,33},{33,1},{2,34},{34,2},{3,35},{35,3},{4,36},{36... | collective-permute-start | bytes 4718600 | tf_op jit(solution)/shard_map/ppermute | solution.py:55
  93.9 8.8 %copy-start.5 = (bf16[128,512]{1,0:T(8,128)(2,1)S(1)}, bf16[128,512]{1,0:T(8,128)(2,1)}, u32[]{:S(2)}) copy-start(bf16[128,512]{1,0:T(8,128)(2,1)} %get-tuple-element.47) | copy-start | bytes 393220
  98.0 14.9 %collective-permute-start.11 = (bf16[512,1024]{1,0:T(8,128)(2,1)S(1)}, bf16[512,1024]{1,0:T(8,128)(2,1)S(1)}, u32[]{:S(2)}, u32[]{:S(2)}) collective-permute-start(bf16[512,1024]{1,0:T(8,128)(2,1)S(1)} %get-tuple-element.43), channel_id=1, source_target_pairs={{0,64},{1,65},{2,66},{3,67},{32,33},{33,34},{34,35},{35,32},{64,12... | collective-permute-start | bytes 3145736 | tf_op jit(solution)/shard_map/ppermute | solution.py:72
  99.0 16.4 %collective-permute-start.12 = (bf16[512,1024]{1,0:T(8,128)(2,1)S(1)}, bf16[512,1024]{1,0:T(8,128)(2,1)S(1)}, u32[]{:S(2)}, u32[]{:S(2)}) collective-permute-start(bf16[512,1024]{1,0:T(8,128)(2,1)S(1)} %get-tuple-element.44), channel_id=1, source_target_pairs={{0,128},{1,129},{2,130},{3,131},{32,34},{33,35},{34,32},{35,33},{6... | collective-permute-start | bytes 3145736 | tf_op jit(solution)/shard_map/ppermute | solution.py:72
  102.1 24.5 %collective-permute-start.13 = (bf16[512,1024]{1,0:T(8,128)(2,1)S(1)}, bf16[512,1024]{1,0:T(8,128)(2,1)S(1)}, u32[]{:S(2)}, u32[]{:S(2)}) collective-permute-start(bf16[512,1024]{1,0:T(8,128)(2,1)S(1)} %get-tuple-element.45), channel_id=1, source_target_pairs={{0,192},{1,193},{2,194},{3,195},{32,35},{33,32},{34,33},{35,34},{6... | collective-permute-start | bytes 3145736 | tf_op jit(solution)/shard_map/ppermute | solution.py:72
  102.7 1.4 collective-permute-start.17
  104.1 24.5 %collective-permute-start.18 = (bf16[64,512]{1,0:T(8,128)(2,1)S(1)}, bf16[64,512]{1,0:T(8,128)(2,1)S(1)}, u32[]{:S(2)}, u32[]{:S(2)}) collective-permute-start(bf16[64,512]{1,0:T(8,128)(2,1)S(1)} %slice.78), channel_id=1, source_target_pairs={{0,2},{1,3},{2,0},{3,1},{4,6},{5,7},{6,4},{7,5},{8,10},{9,11},{10,... | collective-permute-start | bytes 196616 | tf_op jit(solution)/shard_map/ppermute | solution.py:556
  127.6 26.3 %copy-start.4 = (bf16[512,512]{1,0:T(8,128)(2,1)S(1)}, bf16[512,512]{1,0:T(8,128)(2,1)}, u32[]{:S(2)}) copy-start(bf16[512,512]{1,0:T(8,128)(2,1)} %get-tuple-element.50) | copy-start | bytes 1572868
  127.6 7.7 %collective-permute-start.14 = (bf16[128,1024]{1,0:T(8,128)(2,1)S(1)}, bf16[128,1024]{1,0:T(8,128)(2,1)S(1)}, u32[]{:S(2)}, u32[]{:S(2)}) collective-permute-start(bf16[128,1024]{1,0:T(8,128)(2,1)S(1)} %get-tuple-element.52), channel_id=1, source_target_pairs={{0,1},{1,2},{2,3},{3,0},{32,224},{33,225},{34,226},{35,227},{64,65... | collective-permute-start | bytes 786440 | tf_op jit(solution)/shard_map/ppermute | solution.py:72
  128.7 6.5 %collective-permute-start.19 = (bf16[32,512]{1,0:T(8,128)(2,1)S(1)}, bf16[32,512]{1,0:T(8,128)(2,1)S(1)}, u32[]{:S(2)}, u32[]{:S(2)}) collective-permute-start(bf16[32,512]{1,0:T(8,128)(2,1)S(1)} %slice.79), channel_id=1, source_target_pairs={{0,1},{1,0},{2,3},{3,2},{4,5},{5,4},{6,7},{7,6},{8,9},{9,8},{10,11... | collective-permute-start | bytes 98312 | tf_op jit(solution)/shard_map/ppermute | solution.py:561
  130.3 8.5 %collective-permute-start.16 = (bf16[128,1024]{1,0:T(8,128)(2,1)S(1)}, bf16[128,1024]{1,0:T(8,128)(2,1)S(1)}, u32[]{:S(2)}, u32[]{:S(2)}) collective-permute-start(bf16[128,1024]{1,0:T(8,128)(2,1)S(1)} %get-tuple-element.53), channel_id=1, source_target_pairs={{0,3},{1,0},{2,1},{3,2},{32,96},{33,97},{34,98},{35,99},{64,67},{6... | collective-permute-start | bytes 786440 | tf_op jit(solution)/shard_map/ppermute | solution.py:72
  132.1 7.9 %collective-permute-start.15 = (bf16[128,1024]{1,0:T(8,128)(2,1)S(1)}, bf16[128,1024]{1,0:T(8,128)(2,1)S(1)}, u32[]{:S(2)}, u32[]{:S(2)}) collective-permute-start(bf16[128,1024]{1,0:T(8,128)(2,1)S(1)} %get-tuple-element.54), channel_id=1, source_target_pairs={{0,2},{1,3},{2,0},{3,1},{32,160},{33,161},{34,162},{35,163},{64,66... | collective-permute-start | bytes 786440 | tf_op jit(solution)/shard_map/ppermute | solution.py:72
  135.2 14.2 %collective-permute-start.20 = (f32[32,512]{1,0:T(8,128)S(1)}, f32[32,512]{1,0:T(8,128)S(1)}, u32[]{:S(2)}, u32[]{:S(2)}) collective-permute-start(f32[32,512]{1,0:T(8,128)S(1)} %convert_add_fusion.3), channel_id=1, source_target_pairs={{0,128},{64,192},{128,0},{192,64},{1,129},{65,193},{129,1},{193,65... | collective-permute-start | bytes 196616 | tf_op jit(solution)/shard_map/ppermute | solution.py:563
  140.9 19.0 %all-to-all-start = ((bf16[8,64,256]{2,1,0:T(8,128)(2,1)}), bf16[8,64,256]{2,1,0:T(8,128)(2,1)S(1)}, u32[]{:S(2)}, u32[]{:S(2)}) async-start(bf16[8,64,256]{2,1,0:T(8,128)(2,1)} %pad_maximum_fusion), calls=%async_computation | async-start | bytes 524288 | tf_op jit(solution)/shard_map/all_to_all | solution.py:491
  149.4 4.4 %collective-permute-start.21 = (f32[32,512]{1,0:T(8,128)S(1)}, f32[32,512]{1,0:T(8,128)S(1)}, u32[]{:S(2)}, u32[]{:S(2)}) collective-permute-start(f32[32,512]{1,0:T(8,128)S(1)} %add.42), channel_id=1, source_target_pairs={{0,64},{64,0},{128,192},{192,128},{1,65},{65,1},{129,193},{193,129... | collective-permute-start | bytes 196616 | tf_op jit(solution)/shard_map/ppermute | solution.py:566
  (7 other events, 20.8 us)

commit v2 on v1

--- a/solution.py
+++ b/solution.py
@@ -28,7 +28,7 @@
     return jax.ShapeDtypeStruct(dims, dtype)
 
 
-def call(kernel, out_shape, inputs, in_specs, out_specs, scratch=(), name=None, limit=60, flops=0):
+def call(kernel, out_shape, inputs, in_specs, out_specs, scratch=(), name=None, limit=50, flops=0):
     return pl.pallas_call(
         kernel,
         out_shape=out_shape,
@@ -132,6 +132,7 @@
             pltpu.VMEM((2 * cap + extra, width), BF),
             pltpu.SemaphoreType.DMA((5,)),
         ],
+        limit=60,
         name="expert_rows",
     )
 
@@ -178,9 +179,21 @@
     lax.fori_loop(0, outs.shape[1] // CHUNK, step, 0)
 
 
-def preactivations(xs, weights, second):
+def fetch_columns(fetch, source, target, parts=4):
+    rows, step = source.shape[0], source.shape[1] // parts
+    cols = [pl.ds(i * step, step) for i in range(parts)]
+    return [fetch(source.at[:, c], target.at[pl.ds(0, rows), c]) for c in cols]
+
+
+def preactivations(xs, weights, second, arrivals):
     h, rank = second.shape[2], second.shape[1]
-    pre = dot(xs[...], weights[...], NT)
+    step = xs.shape[1] // len(arrivals)
+    pre = None
+    for i, arrival in enumerate(arrivals):
+        arrival.wait()
+        cols = slice(i * step, (i + 1) * step)
+        term = dot(xs[:, cols], weights[:, cols], NT)
+        pre = term if pre is None else pre + term
     low = pre[:, 2 * h :].astype(BF)
     gate = pre[:, :h] + ADAPTER_SCALE * dot(low[:, :rank], second[0])
     up = pre[:, h : 2 * h] + ADAPTER_SCALE * dot(low[:, rank:], second[1])
@@ -203,7 +216,7 @@
     sources = [b.at[pl.ds(0, extra), :] for b in blocks] + list(fars)
     got_first = [fetch(a, packed.at[pl.ds(i * extra, extra), :]) for i, a in enumerate(sources)]
     got_x = [fetch(b.at[pl.ds(extra, cap), :], xs.at[pl.ds(i * cap, cap), :]) for i, b in enumerate(blocks)]
-    got_gate_up = fetch(gate_up, weights.at[pl.ds(0, 2 * h), :])
+    got_gate_up = fetch_columns(fetch, gate_up, weights)
     got_down = fetch(down, down_v)
 
     wait(got_first)
@@ -216,8 +229,7 @@
             weights[2 * h + j * extra : 2 * h + (j + 1) * extra, at] = piece
     save = [start(first, first_out, out_sems.at[8])]
     wait(got_x)
-    got_gate_up.wait()
-    gate, up, low, act = preactivations(xs, weights, second)
+    gate, up, low, act = preactivations(xs, weights, second, got_gate_up)
     gate_v[...] = gate
     up_v[...] = up
     low_v[...] = low
@@ -260,7 +272,7 @@
             pltpu.VMEM((rows, both), BF),
             pltpu.VMEM(((n + 2) * fars[0].shape[0], width), BF),
             pltpu.VMEM((rows, width), BF),
-            pltpu.SemaphoreType.DMA((2 * n + 4,)),
+            pltpu.SemaphoreType.DMA((2 * n + 8,)),
             pltpu.SemaphoreType.DMA((12,)),
         ],
         flops=10**10,
@@ -291,7 +303,8 @@
         place_of[o * N_Y + 2] = (True, o)
     extra = near[0].shape[0] - 2 * cap
     got_x = [fetch(far[o].at[pl.ds(0, cap), :], xs.at[rows_of(o), :]) for o in range(2)]
-    got_weights = [fetch(gate_up, weights.at[pl.ds(0, 2 * h), :]), fetch(first, weights.at[pl.ds(2 * h, 2 * rank), :])]
+    got_first = fetch(first, weights.at[pl.ds(2 * h, 2 * rank), :])
+    got_gate_up = fetch_columns(fetch, gate_up, weights)
     got_down = fetch(down, down_v)
     got_d, got_pre, saved = [], [], []
     for i in range(n):
@@ -312,8 +325,8 @@
         saved.append(start(source, part.at[pl.ds(at, cap), :], out_sems.at[8 + i]))
 
     wait(got_x)
-    wait(got_weights)
-    gate, up, low, act = preactivations(xs, weights, second)
+    got_first.wait()
+    gate, up, low, act = preactivations(xs, weights, second, got_gate_up)
     hidden[...] = act
     for o in range(2):
         to = (o * N_Y + 2) * cap
@@ -474,7 +487,7 @@
 
 
 def first_moves(parts):
-    return [parts[0]] + [crossed(parts[s], s, 0) for s in range(1, len(parts))]
+    return [parts[0]] + [crossed(parts[s], s, 0) for s in (2, 1, 3)]
 
 
 def second_moves(once, n):

time: 163 us -> 160 us (0.982)
  Pallas kernels: 40.8 us -> 38 us
    pallas_call x4, Pallas kernels: 40.8 us -> 38 us  [call(): pl.pallas_call(kernel, out_shape=out_shape, in_specs=in_specs, out_specs=...]
    unnamed x32 -> x30, local copies, waits for them, and re-layouts: 4.64 us -> 4.99 us
where the time goes in v2:
time: 160 us; the launch traced here: 158 us
  waiting for transfers between devices  75.8 us (47%)
  Pallas kernels  38 us (24%)
  starting transfers between devices  33.5 us (21%)
  local copies, waits for them, and re-layouts  5.78 us (4%)
  other arithmetic  2.74 us (2%)
    pallas_call x4, Pallas kernels, call(): pl.pallas_call(kernel, out_shape=out_shape, in_specs=in_specs, out_specs=...  38 us
    ppermute x4, waiting for transfers between devices, ahead(): return lax.ppermute(values, ('y', 'core'), pairs)  27.6 us
    ppermute x6, waiting for transfers between devices, crossed(): return lax.ppermute(values, ('y', 'core', 'x'), pairs)  23.4 us
    ppermute x8, waiting for transfers between devices, swap(): return lax.ppermute(values, 'core', [(0, 1), (1, 0)])  17.5 us
    ppermute x6, starting transfers between devices, crossed(): return lax.ppermute(values, ('y', 'core', 'x'), pairs)  8.5 us
    all_to_all x1, starting transfers between devices, to_tokens(): came = lax.all_to_all(jnp.concatenate(sent, axis=2), 'z', 0, 0, tiled=True)  8.47 us
    ppermute x4, starting transfers between devices, ahead(): return lax.ppermute(values, ('y', 'core'), pairs)  5.6 us
    all_to_all x1, waiting for transfers between devices, to_tokens(): came = lax.all_to_all(jnp.concatenate(sent, axis=2), 'z', 0, 0, tiled=True)  5.19 us
  transfers between devices with their start and end apart: 23, of which 18 were waited for; matrix products, arithmetic and copies ran while one was open for 2% of the time, Pallas kernels for 8%

profile of v2, /device:TPU:8, one launch (start us, length us, event | category | flops | bytes accessed | tf_op | source)
XLA Modules:
  0.0 157.9 jit_solution(17632800297682400452)
XLA Ops:
  1.3 4.8 %expert_rows.1 = (bf16[144,4096]{1,0:T(8,128)(2,1)}, bf16[16,4096]{1,0:T(8,128)(2,1)}, f32[64,1]{1,0:T(8,128)}) custom-call(s32[4]{0:T(128)} %pad_add_fusion.place, bf16[128,4096]{1,0:T(8,128)(2,1)} %tokens.1, bf16[128,4096]{1,0:T(8,128)(2,1)} %cotangent.1, bf16[2,512,512]{2,1,0:T(8,128)(2,1)} %first.1, s32[2,128]{1,0:T(2,128)} %bitcast.34, f32[2,128]{1,0:T(2,128)} %bitcast.35), custom_call_target="tpu_custom_call" | custom-call | tf_op jit(solution)/shard_map/expert_rows/pallas_call | solution.py:32
  6.1 2.3 %collective-permute-start.1 = (bf16[144,4096]{1,0:T(8,128)(2,1)}, bf16[144,4096]{1,0:T(8,128)(2,1)S(1)}, u32[]{:S(2)}, u32[]{:S(2)}) collective-permute-start(bf16[144,4096]{1,0:T(8,128)(2,1)} %get-tuple-element.28.refs_0_), channel_id=1, source_target_pairs={{0,192},{32,96},{64,0},{96,160},{128,64},{160,224},{192,128},{224,... | collective-permute-start | bytes 3538952 | tf_op jit(solution)/shard_map/ppermute | solution.py:61
  8.4 3.3 %collective-permute-start.2 = (bf16[16,4096]{1,0:T(8,128)(2,1)}, bf16[16,4096]{1,0:T(8,128)(2,1)S(1)}, u32[]{:S(2)}, u32[]{:S(2)}) collective-permute-start(bf16[16,4096]{1,0:T(8,128)(2,1)} %get-tuple-element.29), channel_id=1, source_target_pairs={{0,128},{32,160},{64,192},{96,224},{128,0},{160,32},{192,64},{224,... | collective-permute-start | bytes 393224 | tf_op jit(solution)/shard_map/ppermute | solution.py:61
  11.7 27.2 %collective-permute-done.2.refs_6_ = bf16[16,4096]{1,0:T(8,128)(2,1)S(1)} collective-permute-done((bf16[16,4096]{1,0:T(8,128)(2,1)}, bf16[16,4096]{1,0:T(8,128)(2,1)S(1)}, u32[]{:S(2)}, u32[]{:S(2)}) %collective-permute-start.2) | collective-permute-done | bytes 131104 | tf_op jit(solution)/shard_map/ppermute | solution.py:61
  38.9 1.3 collective-permute-done.3.refs_7_
  41.1 2.1 %collective-permute-done.6.refs_5_ = bf16[144,4096]{1,0:T(8,128)(2,1)S(1)} collective-permute-done((bf16[144,4096]{1,0:T(8,128)(2,1)S(1)}, bf16[144,4096]{1,0:T(8,128)(2,1)S(1)}, u32[]{:S(2)}, u32[]{:S(2)}) %collective-permute-start.6) | collective-permute-done | bytes 1179680 | tf_op jit(solution)/shard_map/ppermute | solution.py:55
  43.2 3.4 %collective-permute-done.5.refs_4_ = bf16[144,4096]{1,0:T(8,128)(2,1)S(1)} collective-permute-done((bf16[144,4096]{1,0:T(8,128)(2,1)S(1)}, bf16[144,4096]{1,0:T(8,128)(2,1)S(1)}, u32[]{:S(2)}, u32[]{:S(2)}) %collective-permute-start.5) | collective-permute-done | bytes 1179680 | tf_op jit(solution)/shard_map/ppermute | solution.py:55
  46.8 1.2 copy-done.13
  48.1 11.9 %forward_rows.1 = (f32[384,336]{1,0:T(8,128)S(1)}, f32[384,336]{1,0:T(8,128)S(1)}, bf16[384,128]{1,0:T(8,128)(2,1)S(1)}, bf16[192,4096]{1,0:T(8,128)(2,1)}, bf16...) custom-call(s32[4]{0:T(128)S(1)} %copy-done.2, bf16[144,4096]{1,0:T(8,128)(2,1)S(1)} %copy-done.3, ...), custom_call_target="tpu_custom_call" | custom-call | flops 10000000000 | tf_op jit(solution)/shard_map/forward_rows/pallas_call | solution.py:32
  60.0 1.0 copy-done.5
  61.4 2.6 %collective-permute-done.8.refs_7_ = bf16[128,4096]{1,0:T(8,128)(2,1)S(1)} collective-permute-done((bf16[128,4096]{1,0:T(8,128)(2,1)S(1)}, bf16[128,4096]{1,0:T(8,128)(2,1)S(1)}, u32[]{:S(2)}, u32[]{:S(2)}) %collective-permute-start.8) | collective-permute-done | bytes 1048608 | tf_op jit(solution)/shard_map/ppermute | solution.py:55
  65.0 17.2 %rest_rows.1 = (bf16[128,512]{1,0:T(8,128)(2,1)S(1)}, bf16[512,512]{1,0:T(8,128)(2,1)S(1)}, f32[2,64,336]{2,1,0:T(8,128)}, bf16[320,4096]{1,0:T(8,128)(2,1)}, bf16[320,4096]{1,0:T(8,128)(2,1)}) custom-call(s32[4]{0:T(128)S(1)} %copy-done.2, bf16[144,4096]{1,0:T(8,128)(2,1)} %get-tuple-element.28.refs_0_, bf16[144,4096]{1,0:T(8,128)(2,1)} %copy-done.10, ...), custom_call_target="tpu_custom_call" | custom-call | flops 10000000000 | tf_op jit(solution)/shard_map/rest_rows/pallas_call | solution.py:32
  82.9 6.6 %collective-permute-done.9.refs_2_ = bf16[192,4096]{1,0:T(8,128)(2,1)S(1)} collective-permute-done((bf16[192,4096]{1,0:T(8,128)(2,1)S(1)}, bf16[192,4096]{1,0:T(8,128)(2,1)S(1)}, u32[]{:S(2)}, u32[]{:S(2)}) %collective-permute-start.9) | collective-permute-done | bytes 1572896 | tf_op jit(solution)/shard_map/ppermute | solution.py:55
  89.7 1.7 %copy-done = bf16[320,4096]{1,0:T(8,128)(2,1)S(1)} copy-done((bf16[320,4096]{1,0:T(8,128)(2,1)S(1)}, bf16[320,4096]{1,0:T(8,128)(2,1)}, u32[]{:S(2)}) %copy-start) | copy-done | bytes 2621464
  91.5 4.1 %add_and_pack.1 = (bf16[512,1024]{1,0:T(8,128)(2,1)S(1)}, bf16[512,1024]{1,0:T(8,128)(2,1)S(1)}, bf16[512,1024]{1,0:T(8,128)(2,1)S(1)}, bf16[512,1024]{1,0:T(8,128)(2,1)S(1)}) custom-call(s32[4]{0:T(128)S(1)} %copy-done.2, bf16[192,4096]{1,0:T(8,128)(2,1)S(1)} %copy-done.1, bf16[320,4096]{1,0:T(8,128)(2,1)S(1)} %copy-done, ...), custom_call_target="tpu_custom_call" | custom-call | tf_op jit(solution)/shard_map/add_and_pack/pallas_call | solution.py:32
  95.5 2.3 %collective-permute-start.11 = (bf16[512,1024]{1,0:T(8,128)(2,1)S(1)}, bf16[512,1024]{1,0:T(8,128)(2,1)S(1)}, u32[]{:S(2)}, u32[]{:S(2)}) collective-permute-start(bf16[512,1024]{1,0:T(8,128)(2,1)S(1)} %get-tuple-element.43), channel_id=1, source_target_pairs={{0,128},{1,129},{2,130},{3,131},{32,34},{33,35},{34,32},{35,33},{6... | collective-permute-start | bytes 3145736 | tf_op jit(solution)/shard_map/ppermute | solution.py:72
  97.8 1.3 collective-permute-start.12
  99.9 1.3 collective-permute-start.17
  102.3 2.1 %collective-permute-start.18 = (bf16[64,512]{1,0:T(8,128)(2,1)S(1)}, bf16[64,512]{1,0:T(8,128)(2,1)S(1)}, u32[]{:S(2)}, u32[]{:S(2)}) collective-permute-start(bf16[64,512]{1,0:T(8,128)(2,1)S(1)} %slice.78), channel_id=1, source_target_pairs={{0,2},{1,3},{2,0},{3,1},{4,6},{5,7},{6,4},{7,5},{8,10},{9,11},{10,... | collective-permute-start | bytes 196616 | tf_op jit(solution)/shard_map/ppermute | solution.py:569
  104.4 7.6 %collective-permute-done.11 = bf16[512,1024]{1,0:T(8,128)(2,1)S(1)} collective-permute-done((bf16[512,1024]{1,0:T(8,128)(2,1)S(1)}, bf16[512,1024]{1,0:T(8,128)(2,1)S(1)}, u32[]{:S(2)}, u32[]{:S(2)}) %collective-permute-start.11) | collective-permute-done | bytes 1048608 | tf_op jit(solution)/shard_map/ppermute | solution.py:72
  112.0 10.9 %collective-permute-done.12 = bf16[512,1024]{1,0:T(8,128)(2,1)S(1)} collective-permute-done((bf16[512,1024]{1,0:T(8,128)(2,1)S(1)}, bf16[512,1024]{1,0:T(8,128)(2,1)S(1)}, u32[]{:S(2)}, u32[]{:S(2)}) %collective-permute-start.12) | collective-permute-done | bytes 1048608 | tf_op jit(solution)/shard_map/ppermute | solution.py:72
  124.2 1.6 collective-permute-start.14
  125.8 1.6 collective-permute-start.19
  127.3 1.8 %collective-permute-start.16 = (bf16[128,1024]{1,0:T(8,128)(2,1)S(1)}, bf16[128,1024]{1,0:T(8,128)(2,1)S(1)}, u32[]{:S(2)}, u32[]{:S(2)}) collective-permute-start(bf16[128,1024]{1,0:T(8,128)(2,1)S(1)} %get-tuple-element.53), channel_id=1, source_target_pairs={{0,3},{1,0},{2,1},{3,2},{32,96},{33,97},{34,98},{35,99},{64,67},{6... | collective-permute-start | bytes 786440 | tf_op jit(solution)/shard_map/ppermute | solution.py:72
  130.1 1.7 %collective-permute-done.14 = bf16[128,1024]{1,0:T(8,128)(2,1)S(1)} collective-permute-done((bf16[128,1024]{1,0:T(8,128)(2,1)S(1)}, bf16[128,1024]{1,0:T(8,128)(2,1)S(1)}, u32[]{:S(2)}, u32[]{:S(2)}) %collective-permute-start.14) | collective-permute-done | bytes 262176 | tf_op jit(solution)/shard_map/ppermute | solution.py:72
  131.8 2.3 %collective-permute-start.20 = (f32[32,512]{1,0:T(8,128)S(1)}, f32[32,512]{1,0:T(8,128)S(1)}, u32[]{:S(2)}, u32[]{:S(2)}) collective-permute-start(f32[32,512]{1,0:T(8,128)S(1)} %convert_add_fusion.3), channel_id=1, source_target_pairs={{0,128},{64,192},{128,0},{192,64},{1,129},{65,193},{129,1},{193,65... | collective-permute-start | bytes 196616 | tf_op jit(solution)/shard_map/ppermute | solution.py:576
  134.1 1.7 %collective-permute-done.16 = bf16[128,1024]{1,0:T(8,128)(2,1)S(1)} collective-permute-done((bf16[128,1024]{1,0:T(8,128)(2,1)S(1)}, bf16[128,1024]{1,0:T(8,128)(2,1)S(1)}, u32[]{:S(2)}, u32[]{:S(2)}) %collective-permute-start.16) | collective-permute-done | bytes 262176 | tf_op jit(solution)/shard_map/ppermute | solution.py:72
  135.9 1.1 collective-permute-done.15
  138.0 8.5 %all-to-all-start = ((bf16[8,64,256]{2,1,0:T(8,128)(2,1)}), bf16[8,64,256]{2,1,0:T(8,128)(2,1)S(1)}, u32[]{:S(2)}, u32[]{:S(2)}) async-start(bf16[8,64,256]{2,1,0:T(8,128)(2,1)} %pad_maximum_fusion), calls=%async_computation | async-start | bytes 524288 | tf_op jit(solution)/shard_map/all_to_all | solution.py:504
  146.5 2.2 %collective-permute-start.21 = (f32[32,512]{1,0:T(8,128)S(1)}, f32[32,512]{1,0:T(8,128)S(1)}, u32[]{:S(2)}, u32[]{:S(2)}) collective-permute-start(f32[32,512]{1,0:T(8,128)S(1)} %add.42), channel_id=1, source_target_pairs={{0,64},{64,0},{128,192},{192,128},{1,65},{65,1},{129,193},{193,129... | collective-permute-start | bytes 196616 | tf_op jit(solution)/shard_map/ppermute | solution.py:579
  148.8 2.1 %collective-permute-done.21 = f32[32,512]{1,0:T(8,128)S(1)} collective-permute-done((f32[32,512]{1,0:T(8,128)S(1)}, f32[32,512]{1,0:T(8,128)S(1)}, u32[]{:S(2)}, u32[]{:S(2)}) %collective-permute-start.21) | collective-permute-done | bytes 65568 | tf_op jit(solution)/shard_map/ppermute | solution.py:579
  151.8 5.2 %all-to-all-done = bf16[8,64,256]{2,1,0:T(8,128)(2,1)S(1)} async-done(((bf16[8,64,256]{2,1,0:T(8,128)(2,1)}), bf16[8,64,256]{2,1,0:T(8,128)(2,1)S(1)}, u32[]{:S(2)}, u32[]{:S(2)}) %all-to-all-start) | async-done | bytes 262176 | tf_op jit(solution)/shard_map/all_to_all | solution.py:504
  (69 shorter events, 10.8 us)
Async XLA Ops:
  1.3 46.8 %copy-start.2 = (s32[4]{0:T(128)S(1)}, s32[4]{0:T(128)}, u32[]{:S(2)}) copy-start(s32[4]{0:T(128)} %pad_add_fusion.place) | copy-start | bytes 52
  1.3 46.8 %copy-start.4 = (bf16[2,64,336]{2,1,0:T(8,128)(2,1)S(1)}, bf16[2,64,336]{2,1,0:T(8,128)(2,1)}, u32[]{:S(2)}) copy-start(bf16[2,64,336]{2,1,0:T(8,128)(2,1)} %refs_14_.1) | copy-start | bytes 258052
  6.1 42.0 %copy-start.3 = (bf16[144,4096]{1,0:T(8,128)(2,1)S(1)}, bf16[144,4096]{1,0:T(8,128)(2,1)}, u32[]{:S(2)}) copy-start(bf16[144,4096]{1,0:T(8,128)(2,1)} %get-tuple-element.28.refs_0_) | copy-start | bytes 3538948
  6.1 34.2 %collective-permute-start.1 = (bf16[144,4096]{1,0:T(8,128)(2,1)}, bf16[144,4096]{1,0:T(8,128)(2,1)S(1)}, u32[]{:S(2)}, u32[]{:S(2)}) collective-permute-start(bf16[144,4096]{1,0:T(8,128)(2,1)} %get-tuple-element.28.refs_0_), channel_id=1, source_target_pairs={{0,192},{32,96},{64,0},{96,160},{128,64},{160,224},{192,128},{224,... | collective-permute-start | bytes 3538952 | tf_op jit(solution)/shard_map/ppermute | solution.py:61
  8.4 31.9 %collective-permute-start = (bf16[144,4096]{1,0:T(8,128)(2,1)}, bf16[144,4096]{1,0:T(8,128)(2,1)S(1)}, u32[]{:S(2)}, u32[]{:S(2)}) collective-permute-start(bf16[144,4096]{1,0:T(8,128)(2,1)} %get-tuple-element.28.refs_0_), channel_id=1, source_target_pairs={{0,64},{32,224},{64,128},{96,32},{128,192},{160,96},{192,0},{224,1... | collective-permute-start | bytes 3538952 | tf_op jit(solution)/shard_map/ppermute | solution.py:61
  8.4 30.5 %collective-permute-start.2 = (bf16[16,4096]{1,0:T(8,128)(2,1)}, bf16[16,4096]{1,0:T(8,128)(2,1)S(1)}, u32[]{:S(2)}, u32[]{:S(2)}) collective-permute-start(bf16[16,4096]{1,0:T(8,128)(2,1)} %get-tuple-element.29), channel_id=1, source_target_pairs={{0,128},{32,160},{64,192},{96,224},{128,0},{160,32},{192,64},{224,... | collective-permute-start | bytes 393224 | tf_op jit(solution)/shard_map/ppermute | solution.py:61
  38.9 1.3 collective-permute-start.3
  40.3 7.8 %copy-start.10 = (bf16[144,4096]{1,0:T(8,128)(2,1)}, bf16[144,4096]{1,0:T(8,128)(2,1)S(1)}, u32[]{:S(2)}) copy-start(bf16[144,4096]{1,0:T(8,128)(2,1)S(1)} %collective-permute-done.1.refs_1_) | copy-start | bytes 3538948
  40.3 7.8 %copy-start.6 = (bf16[144,4096]{1,0:T(8,128)(2,1)}, bf16[144,4096]{1,0:T(8,128)(2,1)S(1)}, u32[]{:S(2)}) copy-start(bf16[144,4096]{1,0:T(8,128)(2,1)S(1)} %collective-permute-done.refs_2_) | copy-start | bytes 3538948
  40.3 2.9 %collective-permute-start.6 = (bf16[144,4096]{1,0:T(8,128)(2,1)S(1)}, bf16[144,4096]{1,0:T(8,128)(2,1)S(1)}, u32[]{:S(2)}, u32[]{:S(2)}) collective-permute-start(bf16[144,4096]{1,0:T(8,128)(2,1)S(1)} %collective-permute-done.1.refs_1_), channel_id=1, source_target_pairs={{0,32},{32,0},{1,33},{33,1},{2,34},{34,2},{3,35},{35,3},{4,36},{36... | collective-permute-start | bytes 3538952 | tf_op jit(solution)/shard_map/ppermute | solution.py:55
  40.5 6.1 %collective-permute-start.5 = (bf16[144,4096]{1,0:T(8,128)(2,1)S(1)}, bf16[144,4096]{1,0:T(8,128)(2,1)S(1)}, u32[]{:S(2)}, u32[]{:S(2)}) collective-permute-start(bf16[144,4096]{1,0:T(8,128)(2,1)S(1)} %collective-permute-done.refs_2_), channel_id=1, source_target_pairs={{0,32},{32,0},{1,33},{33,1},{2,34},{34,2},{3,35},{35,3},{4,36},{36... | collective-permute-start | bytes 3538952 | tf_op jit(solution)/shard_map/ppermute | solution.py:55
  40.9 5.9 %collective-permute-start.4 = (bf16[144,4096]{1,0:T(8,128)(2,1)}, bf16[144,4096]{1,0:T(8,128)(2,1)S(1)}, u32[]{:S(2)}, u32[]{:S(2)}) collective-permute-start(bf16[144,4096]{1,0:T(8,128)(2,1)} %get-tuple-element.28.refs_0_), channel_id=1, source_target_pairs={{0,32},{32,0},{1,33},{33,1},{2,34},{34,2},{3,35},{35,3},{4,36},{36... | collective-permute-start | bytes 3538952 | tf_op jit(solution)/shard_map/ppermute | solution.py:55
  46.6 14.8 %collective-permute-start.7 = (bf16[128,4096]{1,0:T(8,128)(2,1)S(1)}, bf16[128,4096]{1,0:T(8,128)(2,1)S(1)}, u32[]{:S(2)}, u32[]{:S(2)}) collective-permute-start(bf16[128,4096]{1,0:T(8,128)(2,1)S(1)} %slice.42), channel_id=1, source_target_pairs={{0,64},{32,224},{64,128},{96,32},{128,192},{160,96},{192,0},{224,1... | collective-permute-start | bytes 3145736 | tf_op jit(solution)/shard_map/ppermute | solution.py:61
  61.4 2.7 %collective-permute-start.8 = (bf16[128,4096]{1,0:T(8,128)(2,1)S(1)}, bf16[128,4096]{1,0:T(8,128)(2,1)S(1)}, u32[]{:S(2)}, u32[]{:S(2)}) collective-permute-start(bf16[128,4096]{1,0:T(8,128)(2,1)S(1)} %collective-permute-done.7.refs_6_), channel_id=1, source_target_pairs={{0,32},{32,0},{1,33},{33,1},{2,34},{34,2},{3,35},{35,3},{4,36},{36... | collective-permute-start | bytes 3145736 | tf_op jit(solution)/shard_map/ppermute | solution.py:55
  65.0 17.5 %copy-start.9 = (bf16[192,4096]{1,0:T(8,128)(2,1)S(1)}, bf16[192,4096]{1,0:T(8,128)(2,1)}, u32[]{:S(2)}) copy-start(bf16[192,4096]{1,0:T(8,128)(2,1)} %get-tuple-element.40) | copy-start | bytes 4718596
  65.0 24.7 %copy-start.1 = (bf16[192,4096]{1,0:T(8,128)(2,1)S(1)}, bf16[192,4096]{1,0:T(8,128)(2,1)}, u32[]{:S(2)}) copy-start(bf16[192,4096]{1,0:T(8,128)(2,1)} %get-tuple-element.32.refs_0_) | copy-start | bytes 4718596
  82.3 7.5 %collective-permute-start.10 = (bf16[320,4096]{1,0:T(8,128)(2,1)}, bf16[320,4096]{1,0:T(8,128)(2,1)S(1)}, u32[]{:S(2)}, u32[]{:S(2)}) collective-permute-start(bf16[320,4096]{1,0:T(8,128)(2,1)} %get-tuple-element.41), channel_id=1, source_target_pairs={{0,32},{32,0},{1,33},{33,1},{2,34},{34,2},{3,35},{35,3},{4,36},{36... | collective-permute-start | bytes 7864328 | tf_op jit(solution)/shard_map/ppermute | solution.py:55
  82.5 6.9 %collective-permute-start.9 = (bf16[192,4096]{1,0:T(8,128)(2,1)S(1)}, bf16[192,4096]{1,0:T(8,128)(2,1)S(1)}, u32[]{:S(2)}, u32[]{:S(2)}) collective-permute-start(bf16[192,4096]{1,0:T(8,128)(2,1)S(1)} %copy-done.9), channel_id=1, source_target_pairs={{0,32},{32,0},{1,33},{33,1},{2,34},{34,2},{3,35},{35,3},{4,36},{36... | collective-permute-start | bytes 4718600 | tf_op jit(solution)/shard_map/ppermute | solution.py:55
  95.5 16.5 %collective-permute-start.11 = (bf16[512,1024]{1,0:T(8,128)(2,1)S(1)}, bf16[512,1024]{1,0:T(8,128)(2,1)S(1)}, u32[]{:S(2)}, u32[]{:S(2)}) collective-permute-start(bf16[512,1024]{1,0:T(8,128)(2,1)S(1)} %get-tuple-element.43), channel_id=1, source_target_pairs={{0,128},{1,129},{2,130},{3,131},{32,34},{33,35},{34,32},{35,33},{6... | collective-permute-start | bytes 3145736 | tf_op jit(solution)/shard_map/ppermute | solution.py:72
  97.8 25.1 %collective-permute-start.12 = (bf16[512,1024]{1,0:T(8,128)(2,1)S(1)}, bf16[512,1024]{1,0:T(8,128)(2,1)S(1)}, u32[]{:S(2)}, u32[]{:S(2)}) collective-permute-start(bf16[512,1024]{1,0:T(8,128)(2,1)S(1)} %get-tuple-element.44), channel_id=1, source_target_pairs={{0,64},{1,65},{2,66},{3,67},{32,33},{33,34},{34,35},{35,32},{64,12... | collective-permute-start | bytes 3145736 | tf_op jit(solution)/shard_map/ppermute | solution.py:72
  99.2 24.0 %collective-permute-start.13 = (bf16[512,1024]{1,0:T(8,128)(2,1)S(1)}, bf16[512,1024]{1,0:T(8,128)(2,1)S(1)}, u32[]{:S(2)}, u32[]{:S(2)}) collective-permute-start(bf16[512,1024]{1,0:T(8,128)(2,1)S(1)} %get-tuple-element.45), channel_id=1, source_target_pairs={{0,192},{1,193},{2,194},{3,195},{32,35},{33,32},{34,33},{35,34},{6... | collective-permute-start | bytes 3145736 | tf_op jit(solution)/shard_map/ppermute | solution.py:72
  99.9 2.3 %collective-permute-start.17 = (bf16[128,512]{1,0:T(8,128)(2,1)S(1)}, bf16[128,512]{1,0:T(8,128)(2,1)S(1)}, u32[]{:S(2)}, u32[]{:S(2)}) collective-permute-start(bf16[128,512]{1,0:T(8,128)(2,1)S(1)} %get-tuple-element.47), channel_id=1, source_target_pairs={{0,32},{32,0},{1,33},{33,1},{2,34},{34,2},{3,35},{35,3},{4,36},{36... | collective-permute-start | bytes 393224 | tf_op jit(solution)/shard_map/ppermute | solution.py:55
  102.3 23.5 %collective-permute-start.18 = (bf16[64,512]{1,0:T(8,128)(2,1)S(1)}, bf16[64,512]{1,0:T(8,128)(2,1)S(1)}, u32[]{:S(2)}, u32[]{:S(2)}) collective-permute-start(bf16[64,512]{1,0:T(8,128)(2,1)S(1)} %slice.78), channel_id=1, source_target_pairs={{0,2},{1,3},{2,0},{3,1},{4,6},{5,7},{6,4},{7,5},{8,10},{9,11},{10,... | collective-permute-start | bytes 196616 | tf_op jit(solution)/shard_map/ppermute | solution.py:569
  123.2 6.8 %copy-start.8 = (s32[128,2]{0,1:T(2,128)S(1)}, s32[128,2]{0,1:T(2,128)}, u32[]{:S(2)}) copy-start(s32[128,2]{0,1:T(2,128)} %param.9) | copy-start | bytes 3076
  123.2 6.8 %copy-start.7 = (f32[64,1]{1,0:T(8,128)S(1)}, f32[64,1]{1,0:T(8,128)}, u32[]{:S(2)}) copy-start(f32[64,1]{1,0:T(8,128)} %get-tuple-element.46) | copy-start | bytes 772
  124.2 7.7 %collective-permute-start.14 = (bf16[128,1024]{1,0:T(8,128)(2,1)S(1)}, bf16[128,1024]{1,0:T(8,128)(2,1)S(1)}, u32[]{:S(2)}, u32[]{:S(2)}) collective-permute-start(bf16[128,1024]{1,0:T(8,128)(2,1)S(1)} %get-tuple-element.52), channel_id=1, source_target_pairs={{0,1},{1,2},{2,3},{3,0},{32,224},{33,225},{34,226},{35,227},{64,65... | collective-permute-start | bytes 786440 | tf_op jit(solution)/shard_map/ppermute | solution.py:72
  125.8 6.1 %collective-permute-start.19 = (bf16[32,512]{1,0:T(8,128)(2,1)S(1)}, bf16[32,512]{1,0:T(8,128)(2,1)S(1)}, u32[]{:S(2)}, u32[]{:S(2)}) collective-permute-start(bf16[32,512]{1,0:T(8,128)(2,1)S(1)} %slice.79), channel_id=1, source_target_pairs={{0,1},{1,0},{2,3},{3,2},{4,5},{5,4},{6,7},{7,6},{8,9},{9,8},{10,11... | collective-permute-start | bytes 98312 | tf_op jit(solution)/shard_map/ppermute | solution.py:574
  127.3 8.5 %collective-permute-start.16 = (bf16[128,1024]{1,0:T(8,128)(2,1)S(1)}, bf16[128,1024]{1,0:T(8,128)(2,1)S(1)}, u32[]{:S(2)}, u32[]{:S(2)}) collective-permute-start(bf16[128,1024]{1,0:T(8,128)(2,1)S(1)} %get-tuple-element.53), channel_id=1, source_target_pairs={{0,3},{1,0},{2,1},{3,2},{32,96},{33,97},{34,98},{35,99},{64,67},{6... | collective-permute-start | bytes 786440 | tf_op jit(solution)/shard_map/ppermute | solution.py:72
  129.1 7.9 %collective-permute-start.15 = (bf16[128,1024]{1,0:T(8,128)(2,1)S(1)}, bf16[128,1024]{1,0:T(8,128)(2,1)S(1)}, u32[]{:S(2)}, u32[]{:S(2)}) collective-permute-start(bf16[128,1024]{1,0:T(8,128)(2,1)S(1)} %get-tuple-element.54), channel_id=1, source_target_pairs={{0,2},{1,3},{2,0},{3,1},{32,160},{33,161},{34,162},{35,163},{64,66... | collective-permute-start | bytes 786440 | tf_op jit(solution)/shard_map/ppermute | solution.py:72
  131.8 14.7 %collective-permute-start.20 = (f32[32,512]{1,0:T(8,128)S(1)}, f32[32,512]{1,0:T(8,128)S(1)}, u32[]{:S(2)}, u32[]{:S(2)}) collective-permute-start(f32[32,512]{1,0:T(8,128)S(1)} %convert_add_fusion.3), channel_id=1, source_target_pairs={{0,128},{64,192},{128,0},{192,64},{1,129},{65,193},{129,1},{193,65... | collective-permute-start | bytes 196616 | tf_op jit(solution)/shard_map/ppermute | solution.py:576
  138.0 19.0 %all-to-all-start = ((bf16[8,64,256]{2,1,0:T(8,128)(2,1)}), bf16[8,64,256]{2,1,0:T(8,128)(2,1)S(1)}, u32[]{:S(2)}, u32[]{:S(2)}) async-start(bf16[8,64,256]{2,1,0:T(8,128)(2,1)} %pad_maximum_fusion), calls=%async_computation | async-start | bytes 524288 | tf_op jit(solution)/shard_map/all_to_all | solution.py:504
  146.5 4.4 %collective-permute-start.21 = (f32[32,512]{1,0:T(8,128)S(1)}, f32[32,512]{1,0:T(8,128)S(1)}, u32[]{:S(2)}, u32[]{:S(2)}) collective-permute-start(f32[32,512]{1,0:T(8,128)S(1)} %add.42), channel_id=1, source_target_pairs={{0,64},{64,0},{128,192},{192,128},{1,65},{65,1},{129,193},{193,129... | collective-permute-start | bytes 196616 | tf_op jit(solution)/shard_map/ppermute | solution.py:579
  (6 other events, 11.2 us)

commit v3 on v2

--- a/solution.py
+++ b/solution.py
@@ -571,8 +571,8 @@
     got = first_moves(parts)
     got_again = second_moves(total(got).astype(BF), n_y)
     pair = tie(low_sum[: 2 * cols], *got) + moved.astype(F32)
-    low_sum = lax.ppermute(pair[cols:].astype(BF), "x", crossing("x", 1)).astype(F32)
-    low_sum = tie(pair[:cols], got_again[1]) + low_sum
+    sent = tie(pair[cols:].astype(BF), got_again[1])
+    low_sum = pair[:cols] + lax.ppermute(sent, "x", crossing("x", 1)).astype(F32)
     low_sum = low_sum + lax.ppermute(low_sum, "y", crossing("y", 2))
     sums = total(got_again)
     mixed, token_gradient = to_tokens([sums[:cap] * row_gate, sums[cap:]], combine)

time: 160 us -> 160 us (level)
  waiting for transfers between devices: 75.8 us -> 78.1 us
  starting transfers between devices: 33.5 us -> 31.4 us
    unnamed x30 -> x28, local copies, waits for them, and re-layouts: 4.99 us -> 4.97 us
  transfers between devices with their start and end apart: 23 -> 23, of which waited for: 18 -> 17; matrix products, arithmetic and copies ran while one was open for 2% -> 2% of each run, Pallas kernels for 8% -> 7%
where the time goes in v3:
time: 160 us; the launch traced here: 159 us
  waiting for transfers between devices  78.1 us (49%)
  Pallas kernels  37.8 us (24%)
  starting transfers between devices  31.4 us (20%)
  local copies, waits for them, and re-layouts  5.77 us (4%)
  other arithmetic  3.44 us (2%)
    pallas_call x4, Pallas kernels, call(): pl.pallas_call(kernel, out_shape=out_shape, in_specs=in_specs, out_specs=...  37.8 us
    ppermute x4, waiting for transfers between devices, ahead(): return lax.ppermute(values, ('y', 'core'), pairs)  27.7 us
    ppermute x6, waiting for transfers between devices, crossed(): return lax.ppermute(values, ('y', 'core', 'x'), pairs)  24.3 us
    ppermute x8, waiting for transfers between devices, swap(): return lax.ppermute(values, 'core', [(0, 1), (1, 0)])  17.5 us
    ppermute x6, starting transfers between devices, crossed(): return lax.ppermute(values, ('y', 'core', 'x'), pairs)  9.35 us
    all_to_all x1, starting transfers between devices, to_tokens(): came = lax.all_to_all(jnp.concatenate(sent, axis=2), 'z', 0, 0, tiled=True)  8.47 us
    ppermute x4, starting transfers between devices, ahead(): return lax.ppermute(values, ('y', 'core'), pairs)  5.62 us
    all_to_all x1, waiting for transfers between devices, to_tokens(): came = lax.all_to_all(jnp.concatenate(sent, axis=2), 'z', 0, 0, tiled=True)  5.28 us
  transfers between devices with their start and end apart: 23, of which 17 were waited for; matrix products, arithmetic and copies ran while one was open for 2% of the time, Pallas kernels for 7%

profile of v3, /device:TPU:8, one launch (start us, length us, event | category | flops | bytes accessed | tf_op | source)
XLA Modules:
  0.0 158.6 jit_solution(16699929107692939460)
XLA Ops:
  1.2 4.8 %expert_rows.1 = (bf16[144,4096]{1,0:T(8,128)(2,1)}, bf16[16,4096]{1,0:T(8,128)(2,1)}, f32[64,1]{1,0:T(8,128)}) custom-call(s32[4]{0:T(128)} %pad_add_fusion.place, bf16[128,4096]{1,0:T(8,128)(2,1)} %tokens.1, bf16[128,4096]{1,0:T(8,128)(2,1)} %cotangent.1, bf16[2,512,512]{2,1,0:T(8,128)(2,1)} %first.1, s32[2,128]{1,0:T(2,128)} %bitcast.34, f32[2,128]{1,0:T(2,128)} %bitcast.35), custom_call_target="tpu_custom_call" | custom-call | tf_op jit(solution)/shard_map/expert_rows/pallas_call | solution.py:32
  6.0 2.3 %collective-permute-start.1 = (bf16[144,4096]{1,0:T(8,128)(2,1)}, bf16[144,4096]{1,0:T(8,128)(2,1)S(1)}, u32[]{:S(2)}, u32[]{:S(2)}) collective-permute-start(bf16[144,4096]{1,0:T(8,128)(2,1)} %get-tuple-element.28.refs_0_), channel_id=1, source_target_pairs={{0,192},{32,96},{64,0},{96,160},{128,64},{160,224},{192,128},{224,... | collective-permute-start | bytes 3538952 | tf_op jit(solution)/shard_map/ppermute | solution.py:61
  8.3 3.3 %collective-permute-start.2 = (bf16[16,4096]{1,0:T(8,128)(2,1)}, bf16[16,4096]{1,0:T(8,128)(2,1)S(1)}, u32[]{:S(2)}, u32[]{:S(2)}) collective-permute-start(bf16[16,4096]{1,0:T(8,128)(2,1)} %get-tuple-element.29), channel_id=1, source_target_pairs={{0,128},{32,160},{64,192},{96,224},{128,0},{160,32},{192,64},{224,... | collective-permute-start | bytes 393224 | tf_op jit(solution)/shard_map/ppermute | solution.py:61
  11.7 27.2 %collective-permute-done.2.refs_6_ = bf16[16,4096]{1,0:T(8,128)(2,1)S(1)} collective-permute-done((bf16[16,4096]{1,0:T(8,128)(2,1)}, bf16[16,4096]{1,0:T(8,128)(2,1)S(1)}, u32[]{:S(2)}, u32[]{:S(2)}) %collective-permute-start.2) | collective-permute-done | bytes 131104 | tf_op jit(solution)/shard_map/ppermute | solution.py:61
  38.9 1.3 collective-permute-done.3.refs_7_
  41.1 2.1 %collective-permute-done.6.refs_5_ = bf16[144,4096]{1,0:T(8,128)(2,1)S(1)} collective-permute-done((bf16[144,4096]{1,0:T(8,128)(2,1)S(1)}, bf16[144,4096]{1,0:T(8,128)(2,1)S(1)}, u32[]{:S(2)}, u32[]{:S(2)}) %collective-permute-start.6) | collective-permute-done | bytes 1179680 | tf_op jit(solution)/shard_map/ppermute | solution.py:55
  43.2 3.4 %collective-permute-done.5.refs_4_ = bf16[144,4096]{1,0:T(8,128)(2,1)S(1)} collective-permute-done((bf16[144,4096]{1,0:T(8,128)(2,1)S(1)}, bf16[144,4096]{1,0:T(8,128)(2,1)S(1)}, u32[]{:S(2)}, u32[]{:S(2)}) %collective-permute-start.5) | collective-permute-done | bytes 1179680 | tf_op jit(solution)/shard_map/ppermute | solution.py:55
  46.8 1.2 copy-done.12
  48.0 11.8 %forward_rows.1 = (f32[384,336]{1,0:T(8,128)S(1)}, f32[384,336]{1,0:T(8,128)S(1)}, bf16[384,128]{1,0:T(8,128)(2,1)S(1)}, bf16[192,4096]{1,0:T(8,128)(2,1)}, bf16...) custom-call(s32[4]{0:T(128)S(1)} %copy-done.2, bf16[144,4096]{1,0:T(8,128)(2,1)S(1)} %copy-done.3, ...), custom_call_target="tpu_custom_call" | custom-call | flops 10000000000 | tf_op jit(solution)/shard_map/forward_rows/pallas_call | solution.py:32
  59.9 1.0 copy-done.5
  61.4 2.7 %collective-permute-done.8.refs_7_ = bf16[128,4096]{1,0:T(8,128)(2,1)S(1)} collective-permute-done((bf16[128,4096]{1,0:T(8,128)(2,1)S(1)}, bf16[128,4096]{1,0:T(8,128)(2,1)S(1)}, u32[]{:S(2)}, u32[]{:S(2)}) %collective-permute-start.8) | collective-permute-done | bytes 1048608 | tf_op jit(solution)/shard_map/ppermute | solution.py:55
  65.0 17.2 %rest_rows.1 = (bf16[128,512]{1,0:T(8,128)(2,1)S(1)}, bf16[512,512]{1,0:T(8,128)(2,1)S(1)}, f32[2,64,336]{2,1,0:T(8,128)}, bf16[320,4096]{1,0:T(8,128)(2,1)}, bf16[320,4096]{1,0:T(8,128)(2,1)}) custom-call(s32[4]{0:T(128)S(1)} %copy-done.2, bf16[144,4096]{1,0:T(8,128)(2,1)} %get-tuple-element.28.refs_0_, bf16[144,4096]{1,0:T(8,128)(2,1)} %copy-done.9, ...), custom_call_target="tpu_custom_call" | custom-call | flops 10000000000 | tf_op jit(solution)/shard_map/rest_rows/pallas_call | solution.py:32
  82.8 6.6 %collective-permute-done.9.refs_2_ = bf16[192,4096]{1,0:T(8,128)(2,1)S(1)} collective-permute-done((bf16[192,4096]{1,0:T(8,128)(2,1)S(1)}, bf16[192,4096]{1,0:T(8,128)(2,1)S(1)}, u32[]{:S(2)}, u32[]{:S(2)}) %collective-permute-start.9) | collective-permute-done | bytes 1572896 | tf_op jit(solution)/shard_map/ppermute | solution.py:55
  89.6 1.7 %copy-done = bf16[320,4096]{1,0:T(8,128)(2,1)S(1)} copy-done((bf16[320,4096]{1,0:T(8,128)(2,1)S(1)}, bf16[320,4096]{1,0:T(8,128)(2,1)}, u32[]{:S(2)}) %copy-start) | copy-done | bytes 2621464
  91.4 4.1 %add_and_pack.1 = (bf16[512,1024]{1,0:T(8,128)(2,1)S(1)}, bf16[512,1024]{1,0:T(8,128)(2,1)S(1)}, bf16[512,1024]{1,0:T(8,128)(2,1)S(1)}, bf16[512,1024]{1,0:T(8,128)(2,1)S(1)}) custom-call(s32[4]{0:T(128)S(1)} %copy-done.2, bf16[192,4096]{1,0:T(8,128)(2,1)S(1)} %copy-done.1, bf16[320,4096]{1,0:T(8,128)(2,1)S(1)} %copy-done, ...), custom_call_target="tpu_custom_call" | custom-call | tf_op jit(solution)/shard_map/add_and_pack/pallas_call | solution.py:32
  95.5 2.2 %collective-permute-start.11 = (bf16[512,1024]{1,0:T(8,128)(2,1)S(1)}, bf16[512,1024]{1,0:T(8,128)(2,1)S(1)}, u32[]{:S(2)}, u32[]{:S(2)}) collective-permute-start(bf16[512,1024]{1,0:T(8,128)(2,1)S(1)} %get-tuple-element.43), channel_id=1, source_target_pairs={{0,128},{1,129},{2,130},{3,131},{32,34},{33,35},{34,32},{35,33},{6... | collective-permute-start | bytes 3145736 | tf_op jit(solution)/shard_map/ppermute | solution.py:72
  97.6 1.5 collective-permute-start.12
  99.7 1.5 collective-permute-start.17
  101.1 1.0 collective-permute-done.17
  102.2 2.0 %collective-permute-start.18 = (bf16[64,512]{1,0:T(8,128)(2,1)S(1)}, bf16[64,512]{1,0:T(8,128)(2,1)S(1)}, u32[]{:S(2)}, u32[]{:S(2)}) collective-permute-start(bf16[64,512]{1,0:T(8,128)(2,1)S(1)} %slice.79), channel_id=1, source_target_pairs={{0,2},{1,3},{2,0},{3,1},{4,6},{5,7},{6,4},{7,5},{8,10},{9,11},{10,... | collective-permute-start | bytes 196616 | tf_op jit(solution)/shard_map/ppermute | solution.py:569
  104.2 7.8 %collective-permute-done.11 = bf16[512,1024]{1,0:T(8,128)(2,1)S(1)} collective-permute-done((bf16[512,1024]{1,0:T(8,128)(2,1)S(1)}, bf16[512,1024]{1,0:T(8,128)(2,1)S(1)}, u32[]{:S(2)}, u32[]{:S(2)}) %collective-permute-start.11) | collective-permute-done | bytes 1048608 | tf_op jit(solution)/shard_map/ppermute | solution.py:72
  111.9 10.8 %collective-permute-done.12 = bf16[512,1024]{1,0:T(8,128)(2,1)S(1)} collective-permute-done((bf16[512,1024]{1,0:T(8,128)(2,1)S(1)}, bf16[512,1024]{1,0:T(8,128)(2,1)S(1)}, u32[]{:S(2)}, u32[]{:S(2)}) %collective-permute-start.12) | collective-permute-done | bytes 1048608 | tf_op jit(solution)/shard_map/ppermute | solution.py:72
  124.1 1.6 collective-permute-start.14
  125.6 1.7 %collective-permute-start.16 = (bf16[128,1024]{1,0:T(8,128)(2,1)S(1)}, bf16[128,1024]{1,0:T(8,128)(2,1)S(1)}, u32[]{:S(2)}, u32[]{:S(2)}) collective-permute-start(bf16[128,1024]{1,0:T(8,128)(2,1)S(1)} %get-tuple-element.53), channel_id=1, source_target_pairs={{0,3},{1,0},{2,1},{3,2},{32,96},{33,97},{34,98},{35,99},{64,67},{6... | collective-permute-start | bytes 786440 | tf_op jit(solution)/shard_map/ppermute | solution.py:72
  127.4 1.8 %collective-permute-start.15 = (bf16[128,1024]{1,0:T(8,128)(2,1)S(1)}, bf16[128,1024]{1,0:T(8,128)(2,1)S(1)}, u32[]{:S(2)}, u32[]{:S(2)}) collective-permute-start(bf16[128,1024]{1,0:T(8,128)(2,1)S(1)} %get-tuple-element.54), channel_id=1, source_target_pairs={{0,2},{1,3},{2,0},{3,1},{32,160},{33,161},{34,162},{35,163},{64,66... | collective-permute-start | bytes 786440 | tf_op jit(solution)/shard_map/ppermute | solution.py:72
  130.2 1.6 collective-permute-done.14
  132.0 3.9 %collective-permute-done.15 = bf16[128,1024]{1,0:T(8,128)(2,1)S(1)} collective-permute-done((bf16[128,1024]{1,0:T(8,128)(2,1)S(1)}, bf16[128,1024]{1,0:T(8,128)(2,1)S(1)}, u32[]{:S(2)}, u32[]{:S(2)}) %collective-permute-start.15) | collective-permute-done | bytes 262176 | tf_op jit(solution)/shard_map/ppermute | solution.py:72
  136.2 1.8 %collective-permute-start.20 = (f32[32,512]{1,0:T(8,128)S(1)}, f32[32,512]{1,0:T(8,128)S(1)}, u32[]{:S(2)}, u32[]{:S(2)}) collective-permute-start(f32[32,512]{1,0:T(8,128)S(1)} %slice_add_fusion), channel_id=1, source_target_pairs={{0,128},{64,192},{128,0},{192,64},{1,129},{65,193},{129,1},{193,65... | collective-permute-start | bytes 196616 | tf_op jit(solution)/shard_map/ppermute | solution.py:576
  138.7 8.5 %all-to-all-start = ((bf16[8,64,256]{2,1,0:T(8,128)(2,1)}), bf16[8,64,256]{2,1,0:T(8,128)(2,1)S(1)}, u32[]{:S(2)}, u32[]{:S(2)}) async-start(bf16[8,64,256]{2,1,0:T(8,128)(2,1)} %pad_maximum_fusion), calls=%async_computation | async-start | bytes 524288 | tf_op jit(solution)/shard_map/all_to_all | solution.py:504
  147.2 1.0 collective-permute-start.21
  148.4 3.2 %collective-permute-done.21 = f32[32,512]{1,0:T(8,128)S(1)} collective-permute-done((f32[32,512]{1,0:T(8,128)S(1)}, f32[32,512]{1,0:T(8,128)S(1)}, u32[]{:S(2)}, u32[]{:S(2)}) %collective-permute-start.21) | collective-permute-done | bytes 65568 | tf_op jit(solution)/shard_map/ppermute | solution.py:579
  152.4 5.3 %all-to-all-done = bf16[8,64,256]{2,1,0:T(8,128)(2,1)S(1)} async-done(((bf16[8,64,256]{2,1,0:T(8,128)(2,1)}), bf16[8,64,256]{2,1,0:T(8,128)(2,1)S(1)}, u32[]{:S(2)}, u32[]{:S(2)}) %all-to-all-start) | async-done | bytes 262176 | tf_op jit(solution)/shard_map/all_to_all | solution.py:504
  (66 shorter events, 10.0 us)
Async XLA Ops:
  1.2 46.8 %copy-start.2 = (s32[4]{0:T(128)S(1)}, s32[4]{0:T(128)}, u32[]{:S(2)}) copy-start(s32[4]{0:T(128)} %pad_add_fusion.place) | copy-start | bytes 52
  1.2 46.8 %copy-start.4 = (bf16[2,64,336]{2,1,0:T(8,128)(2,1)S(1)}, bf16[2,64,336]{2,1,0:T(8,128)(2,1)}, u32[]{:S(2)}) copy-start(bf16[2,64,336]{2,1,0:T(8,128)(2,1)} %refs_14_.1) | copy-start | bytes 258052
  6.0 42.0 %copy-start.3 = (bf16[144,4096]{1,0:T(8,128)(2,1)S(1)}, bf16[144,4096]{1,0:T(8,128)(2,1)}, u32[]{:S(2)}) copy-start(bf16[144,4096]{1,0:T(8,128)(2,1)} %get-tuple-element.28.refs_0_) | copy-start | bytes 3538948
  6.0 34.2 %collective-permute-start.1 = (bf16[144,4096]{1,0:T(8,128)(2,1)}, bf16[144,4096]{1,0:T(8,128)(2,1)S(1)}, u32[]{:S(2)}, u32[]{:S(2)}) collective-permute-start(bf16[144,4096]{1,0:T(8,128)(2,1)} %get-tuple-element.28.refs_0_), channel_id=1, source_target_pairs={{0,192},{32,96},{64,0},{96,160},{128,64},{160,224},{192,128},{224,... | collective-permute-start | bytes 3538952 | tf_op jit(solution)/shard_map/ppermute | solution.py:61
  8.3 31.9 %collective-permute-start = (bf16[144,4096]{1,0:T(8,128)(2,1)}, bf16[144,4096]{1,0:T(8,128)(2,1)S(1)}, u32[]{:S(2)}, u32[]{:S(2)}) collective-permute-start(bf16[144,4096]{1,0:T(8,128)(2,1)} %get-tuple-element.28.refs_0_), channel_id=1, source_target_pairs={{0,64},{32,224},{64,128},{96,32},{128,192},{160,96},{192,0},{224,1... | collective-permute-start | bytes 3538952 | tf_op jit(solution)/shard_map/ppermute | solution.py:61
  8.3 30.6 %collective-permute-start.2 = (bf16[16,4096]{1,0:T(8,128)(2,1)}, bf16[16,4096]{1,0:T(8,128)(2,1)S(1)}, u32[]{:S(2)}, u32[]{:S(2)}) collective-permute-start(bf16[16,4096]{1,0:T(8,128)(2,1)} %get-tuple-element.29), channel_id=1, source_target_pairs={{0,128},{32,160},{64,192},{96,224},{128,0},{160,32},{192,64},{224,... | collective-permute-start | bytes 393224 | tf_op jit(solution)/shard_map/ppermute | solution.py:61
  38.9 1.3 collective-permute-start.3
  40.2 7.8 %copy-start.9 = (bf16[144,4096]{1,0:T(8,128)(2,1)}, bf16[144,4096]{1,0:T(8,128)(2,1)S(1)}, u32[]{:S(2)}) copy-start(bf16[144,4096]{1,0:T(8,128)(2,1)S(1)} %collective-permute-done.1.refs_1_) | copy-start | bytes 3538948
  40.2 7.8 %copy-start.6 = (bf16[144,4096]{1,0:T(8,128)(2,1)}, bf16[144,4096]{1,0:T(8,128)(2,1)S(1)}, u32[]{:S(2)}) copy-start(bf16[144,4096]{1,0:T(8,128)(2,1)S(1)} %collective-permute-done.refs_2_) | copy-start | bytes 3538948
  40.2 2.9 %collective-permute-start.6 = (bf16[144,4096]{1,0:T(8,128)(2,1)S(1)}, bf16[144,4096]{1,0:T(8,128)(2,1)S(1)}, u32[]{:S(2)}, u32[]{:S(2)}) collective-permute-start(bf16[144,4096]{1,0:T(8,128)(2,1)S(1)} %collective-permute-done.1.refs_1_), channel_id=1, source_target_pairs={{0,32},{32,0},{1,33},{33,1},{2,34},{34,2},{3,35},{35,3},{4,36},{36... | collective-permute-start | bytes 3538952 | tf_op jit(solution)/shard_map/ppermute | solution.py:55
  40.5 6.1 %collective-permute-start.5 = (bf16[144,4096]{1,0:T(8,128)(2,1)S(1)}, bf16[144,4096]{1,0:T(8,128)(2,1)S(1)}, u32[]{:S(2)}, u32[]{:S(2)}) collective-permute-start(bf16[144,4096]{1,0:T(8,128)(2,1)S(1)} %collective-permute-done.refs_2_), channel_id=1, source_target_pairs={{0,32},{32,0},{1,33},{33,1},{2,34},{34,2},{3,35},{35,3},{4,36},{36... | collective-permute-start | bytes 3538952 | tf_op jit(solution)/shard_map/ppermute | solution.py:55
  40.8 5.9 %collective-permute-start.4 = (bf16[144,4096]{1,0:T(8,128)(2,1)}, bf16[144,4096]{1,0:T(8,128)(2,1)S(1)}, u32[]{:S(2)}, u32[]{:S(2)}) collective-permute-start(bf16[144,4096]{1,0:T(8,128)(2,1)} %get-tuple-element.28.refs_0_), channel_id=1, source_target_pairs={{0,32},{32,0},{1,33},{33,1},{2,34},{34,2},{3,35},{35,3},{4,36},{36... | collective-permute-start | bytes 3538952 | tf_op jit(solution)/shard_map/ppermute | solution.py:55
  43.2 4.8 %copy-start.10 = (bf16[144,4096]{1,0:T(8,128)(2,1)}, bf16[144,4096]{1,0:T(8,128)(2,1)S(1)}, u32[]{:S(2)}) copy-start(bf16[144,4096]{1,0:T(8,128)(2,1)S(1)} %collective-permute-done.6.refs_5_) | copy-start | bytes 3538948
  46.5 14.8 %collective-permute-start.7 = (bf16[128,4096]{1,0:T(8,128)(2,1)S(1)}, bf16[128,4096]{1,0:T(8,128)(2,1)S(1)}, u32[]{:S(2)}, u32[]{:S(2)}) collective-permute-start(bf16[128,4096]{1,0:T(8,128)(2,1)S(1)} %slice.42), channel_id=1, source_target_pairs={{0,64},{32,224},{64,128},{96,32},{128,192},{160,96},{192,0},{224,1... | collective-permute-start | bytes 3145736 | tf_op jit(solution)/shard_map/ppermute | solution.py:61
  61.3 2.7 %collective-permute-start.8 = (bf16[128,4096]{1,0:T(8,128)(2,1)S(1)}, bf16[128,4096]{1,0:T(8,128)(2,1)S(1)}, u32[]{:S(2)}, u32[]{:S(2)}) collective-permute-start(bf16[128,4096]{1,0:T(8,128)(2,1)S(1)} %collective-permute-done.7.refs_6_), channel_id=1, source_target_pairs={{0,32},{32,0},{1,33},{33,1},{2,34},{34,2},{3,35},{35,3},{4,36},{36... | collective-permute-start | bytes 3145736 | tf_op jit(solution)/shard_map/ppermute | solution.py:55
  65.0 17.4 %copy-start.8 = (bf16[192,4096]{1,0:T(8,128)(2,1)S(1)}, bf16[192,4096]{1,0:T(8,128)(2,1)}, u32[]{:S(2)}) copy-start(bf16[192,4096]{1,0:T(8,128)(2,1)} %get-tuple-element.40) | copy-start | bytes 4718596
  65.0 24.7 %copy-start.1 = (bf16[192,4096]{1,0:T(8,128)(2,1)S(1)}, bf16[192,4096]{1,0:T(8,128)(2,1)}, u32[]{:S(2)}) copy-start(bf16[192,4096]{1,0:T(8,128)(2,1)} %get-tuple-element.32.refs_0_) | copy-start | bytes 4718596
  82.2 7.5 %collective-permute-start.10 = (bf16[320,4096]{1,0:T(8,128)(2,1)}, bf16[320,4096]{1,0:T(8,128)(2,1)S(1)}, u32[]{:S(2)}, u32[]{:S(2)}) collective-permute-start(bf16[320,4096]{1,0:T(8,128)(2,1)} %get-tuple-element.41), channel_id=1, source_target_pairs={{0,32},{32,0},{1,33},{33,1},{2,34},{34,2},{3,35},{35,3},{4,36},{36... | collective-permute-start | bytes 7864328 | tf_op jit(solution)/shard_map/ppermute | solution.py:55
  82.4 6.9 %collective-permute-start.9 = (bf16[192,4096]{1,0:T(8,128)(2,1)S(1)}, bf16[192,4096]{1,0:T(8,128)(2,1)S(1)}, u32[]{:S(2)}, u32[]{:S(2)}) collective-permute-start(bf16[192,4096]{1,0:T(8,128)(2,1)S(1)} %copy-done.8), channel_id=1, source_target_pairs={{0,32},{32,0},{1,33},{33,1},{2,34},{34,2},{3,35},{35,3},{4,36},{36... | collective-permute-start | bytes 4718600 | tf_op jit(solution)/shard_map/ppermute | solution.py:55
  95.5 16.5 %collective-permute-start.11 = (bf16[512,1024]{1,0:T(8,128)(2,1)S(1)}, bf16[512,1024]{1,0:T(8,128)(2,1)S(1)}, u32[]{:S(2)}, u32[]{:S(2)}) collective-permute-start(bf16[512,1024]{1,0:T(8,128)(2,1)S(1)} %get-tuple-element.43), channel_id=1, source_target_pairs={{0,128},{1,129},{2,130},{3,131},{32,34},{33,35},{34,32},{35,33},{6... | collective-permute-start | bytes 3145736 | tf_op jit(solution)/shard_map/ppermute | solution.py:72
  97.6 25.1 %collective-permute-start.12 = (bf16[512,1024]{1,0:T(8,128)(2,1)S(1)}, bf16[512,1024]{1,0:T(8,128)(2,1)S(1)}, u32[]{:S(2)}, u32[]{:S(2)}) collective-permute-start(bf16[512,1024]{1,0:T(8,128)(2,1)S(1)} %get-tuple-element.44), channel_id=1, source_target_pairs={{0,64},{1,65},{2,66},{3,67},{32,33},{33,34},{34,35},{35,32},{64,12... | collective-permute-start | bytes 3145736 | tf_op jit(solution)/shard_map/ppermute | solution.py:72
  99.1 24.0 %collective-permute-start.13 = (bf16[512,1024]{1,0:T(8,128)(2,1)S(1)}, bf16[512,1024]{1,0:T(8,128)(2,1)S(1)}, u32[]{:S(2)}, u32[]{:S(2)}) collective-permute-start(bf16[512,1024]{1,0:T(8,128)(2,1)S(1)} %get-tuple-element.45), channel_id=1, source_target_pairs={{0,192},{1,193},{2,194},{3,195},{32,35},{33,32},{34,33},{35,34},{6... | collective-permute-start | bytes 3145736 | tf_op jit(solution)/shard_map/ppermute | solution.py:72
  99.7 2.4 %collective-permute-start.17 = (bf16[128,512]{1,0:T(8,128)(2,1)S(1)}, bf16[128,512]{1,0:T(8,128)(2,1)S(1)}, u32[]{:S(2)}, u32[]{:S(2)}) collective-permute-start(bf16[128,512]{1,0:T(8,128)(2,1)S(1)} %get-tuple-element.47), channel_id=1, source_target_pairs={{0,32},{32,0},{1,33},{33,1},{2,34},{34,2},{3,35},{35,3},{4,36},{36... | collective-permute-start | bytes 393224 | tf_op jit(solution)/shard_map/ppermute | solution.py:55
  102.2 27.9 %collective-permute-start.18 = (bf16[64,512]{1,0:T(8,128)(2,1)S(1)}, bf16[64,512]{1,0:T(8,128)(2,1)S(1)}, u32[]{:S(2)}, u32[]{:S(2)}) collective-permute-start(bf16[64,512]{1,0:T(8,128)(2,1)S(1)} %slice.79), channel_id=1, source_target_pairs={{0,2},{1,3},{2,0},{3,1},{4,6},{5,7},{6,4},{7,5},{8,10},{9,11},{10,... | collective-permute-start | bytes 196616 | tf_op jit(solution)/shard_map/ppermute | solution.py:569
  123.1 6.1 %copy-start.7 = (s32[128,2]{0,1:T(2,128)S(1)}, s32[128,2]{0,1:T(2,128)}, u32[]{:S(2)}) copy-start(s32[128,2]{0,1:T(2,128)} %param.9) | copy-start | bytes 3076
  124.1 7.7 %collective-permute-start.14 = (bf16[128,1024]{1,0:T(8,128)(2,1)S(1)}, bf16[128,1024]{1,0:T(8,128)(2,1)S(1)}, u32[]{:S(2)}, u32[]{:S(2)}) collective-permute-start(bf16[128,1024]{1,0:T(8,128)(2,1)S(1)} %get-tuple-element.52), channel_id=1, source_target_pairs={{0,1},{1,2},{2,3},{3,0},{32,224},{33,225},{34,226},{35,227},{64,65... | collective-permute-start | bytes 786440 | tf_op jit(solution)/shard_map/ppermute | solution.py:72
  125.6 6.4 %collective-permute-start.16 = (bf16[128,1024]{1,0:T(8,128)(2,1)S(1)}, bf16[128,1024]{1,0:T(8,128)(2,1)S(1)}, u32[]{:S(2)}, u32[]{:S(2)}) collective-permute-start(bf16[128,1024]{1,0:T(8,128)(2,1)S(1)} %get-tuple-element.53), channel_id=1, source_target_pairs={{0,3},{1,0},{2,1},{3,2},{32,96},{33,97},{34,98},{35,99},{64,67},{6... | collective-permute-start | bytes 786440 | tf_op jit(solution)/shard_map/ppermute | solution.py:72
  127.4 8.5 %collective-permute-start.15 = (bf16[128,1024]{1,0:T(8,128)(2,1)S(1)}, bf16[128,1024]{1,0:T(8,128)(2,1)S(1)}, u32[]{:S(2)}, u32[]{:S(2)}) collective-permute-start(bf16[128,1024]{1,0:T(8,128)(2,1)S(1)} %get-tuple-element.54), channel_id=1, source_target_pairs={{0,2},{1,3},{2,0},{3,1},{32,160},{33,161},{34,162},{35,163},{64,66... | collective-permute-start | bytes 786440 | tf_op jit(solution)/shard_map/ppermute | solution.py:72
  131.7 4.4 %collective-permute-start.19 = (bf16[32,512]{1,0:T(8,128)(2,1)S(1)}, bf16[32,512]{1,0:T(8,128)(2,1)S(1)}, u32[]{:S(2)}, u32[]{:S(2)}) collective-permute-start(bf16[32,512]{1,0:T(8,128)(2,1)S(1)} %slice.80), channel_id=1, source_target_pairs={{0,1},{1,0},{2,3},{3,2},{4,5},{5,4},{6,7},{7,6},{8,9},{9,8},{10,11... | collective-permute-start | bytes 98312 | tf_op jit(solution)/shard_map/ppermute | solution.py:575
  136.2 11.0 %collective-permute-start.20 = (f32[32,512]{1,0:T(8,128)S(1)}, f32[32,512]{1,0:T(8,128)S(1)}, u32[]{:S(2)}, u32[]{:S(2)}) collective-permute-start(f32[32,512]{1,0:T(8,128)S(1)} %slice_add_fusion), channel_id=1, source_target_pairs={{0,128},{64,192},{128,0},{192,64},{1,129},{65,193},{129,1},{193,65... | collective-permute-start | bytes 196616 | tf_op jit(solution)/shard_map/ppermute | solution.py:576
  138.7 19.0 %all-to-all-start = ((bf16[8,64,256]{2,1,0:T(8,128)(2,1)}), bf16[8,64,256]{2,1,0:T(8,128)(2,1)S(1)}, u32[]{:S(2)}, u32[]{:S(2)}) async-start(bf16[8,64,256]{2,1,0:T(8,128)(2,1)} %pad_maximum_fusion), calls=%async_computation | async-start | bytes 524288 | tf_op jit(solution)/shard_map/all_to_all | solution.py:504
  147.2 4.4 %collective-permute-start.21 = (f32[32,512]{1,0:T(8,128)S(1)}, f32[32,512]{1,0:T(8,128)S(1)}, u32[]{:S(2)}, u32[]{:S(2)}) collective-permute-start(f32[32,512]{1,0:T(8,128)S(1)} %add.42), channel_id=1, source_target_pairs={{0,64},{64,0},{128,192},{192,128},{1,65},{65,1},{129,193},{193,129... | collective-permute-start | bytes 196616 | tf_op jit(solution)/shard_map/ppermute | solution.py:579
  (5 other events, 6.4 us)
